TPU v7x, 256 devices: a whole 4x4x8 slice. The times are simulated.
256 devices in a mesh: blk: 64 (over z, x, core), mpo: 4 (over y).
Axes of the slice: x: 4, y: 4, z: 8, core: 2. Of those that a mesh axis runs over, the one named last changes fastest.
Arguments:
- psi: bfloat16 [16, 64, 4, 128, 128], P(None, 'blk'), may hold values from -60 to 60, as said below
- left_env: bfloat16 [64, 32, 128, 128], P('blk'), may hold values from -4 to 4, as said below
- right_env: bfloat16 [64, 32, 128, 128], P('blk'), may hold values from -4 to 4, as said below
- live_count: int32 [64], P('blk'), may hold values from 1 to 4, as said below
- right_sector: int32 [64, 4], P('blk'), may hold values from 0 to 63, as said below
- pattern: int32 [32, 2], P('mpo'), may hold values from 0 to 31, as said below
- term_op: bfloat16 [32, 16, 16], P('mpo'), may hold values from -1 to 1, as said below
Outputs:
- applied: bfloat16 [16, 64, 4, 128, 128], P('mpo', 'blk')
- residual: bfloat16 [16, 64, 4, 128, 128], P('mpo', 'blk')
- energy: float32 [], replicated
Inputs may be any that keep to these rules, and one draw needn't show every extreme that they name: psi entries lie between the bounds. `left_env`: environment entries lie between the bounds. `right_env`: environment entries lie between the bounds. `live_count`: some sector has all 4 blocks live. `right_sector`: the right sectors of one left sector l are distinct and lie within 3 of l. pattern[t, 0] lies in 0 to 31; for a term t of group g = t // 8, pattern[t, 1] lies in g * 8 to (g + 1) * 8 - 1. `term_op`: operator entries lie between the bounds.
All inputs are finite; a program needn't handle non-finite values.
Results may differ from a plain program's by a relative error of at most 0.015.
Values may be sent and summed in bfloat16 or wider, within the bound.
No kernel may reach another device: no remote copies, remote signals or barrier semaphores. Data moves between devices by JAX's collectives and lax.ppermute only.
A program may use at most 128 MiB of HBM per device.

v0:
```python
import functools

import jax
import jax.numpy as jnp
from jax import lax
from jax.experimental import pallas as pl
from jax.experimental.pallas import tpu as pltpu
from jax.sharding import PartitionSpec as P

PIECE = ((6, 2, 4, 0, 1, 3, 5), (4, 2, 1, 0, 5, 3, 6))
TERMS = 8
PHYS = 16
SLOTS = 4
TILE = 128
QUARTER = 4


def shift(value, axis, steps):
    count = lax.axis_size(axis)
    return lax.ppermute(value, axis, [(s, (s + steps) % count) for s in range(count)])


def swap(value):
    return lax.ppermute(value, "blk", [(s, s ^ 1) for s in range(lax.axis_size("blk"))])


def neighbours(own):
    count = lax.axis_size("blk")
    odd = lax.axis_index("blk") % 2 == 1
    below = shift(own, "blk", 2)
    above = shift(own, "blk", -2)
    other = swap(own)
    far = jnp.where(odd, below, above)
    far = lax.ppermute(
        far, "blk", [(s, (s + 2) % count if s % 2 else (s - 2) % count) for s in range(count)]
    )
    return own, other, below, above, swap(below), swap(above), swap(far)


def total(value):
    def ring(value, moves):
        moved = [lax.ppermute(value, "blk", [(s, f(s)) for s in range(64)]) for f in moves]
        return functools.reduce(jnp.add, moved, value)

    def along_x(steps):
        return lambda s: (s // 8) * 8 + (s + 2 * steps) % 8

    def along_z(steps):
        return lambda s: (s + 8 * steps) % 64

    value = value + swap(value)
    value = ring(value, [lambda s: s ^ 8])
    value = ring(value, [along_z(2), along_z(4), along_z(6)])
    value = ring(value, [along_x(1), along_x(2), along_x(3)])
    moved = [shift(value, "mpo", d) for d in (1, 2, 3)]
    return functools.reduce(jnp.add, moved, value)


def kernel(scalars, mixed, left, psi, p0, p1, p2, p3, p4, p5, p6, o0, o1, o2, o3, sums, part, right):
    slot = pl.program_id(0)
    pieces = (p0, p1, p2, p3, p4, p5, p6)
    outs = (o0, o1, o2, o3)
    which = scalars[16 + slot]
    for k in range(7):

        @pl.when(which == k)
        def _():
            for t in range(TERMS):
                right[:, t * TILE : (t + 1) * TILE] = pieces[k][scalars[8 + t]]

    for t in range(TERMS):
        factor = left[scalars[t]]
        for p in range(0, PHYS, 4):
            columns = jnp.concatenate([mixed[0, t, p + i] for i in range(4)], 1)
            product = jnp.dot(factor, columns, preferred_element_type=jnp.float32)
            product = product.astype(jnp.bfloat16)
            for i in range(4):
                part[p + i, :, t * TILE : (t + 1) * TILE] = product[:, i * TILE : (i + 1) * TILE]

    numerator = jnp.zeros((TILE, TILE), jnp.float32)
    denominator = jnp.zeros((TILE, TILE), jnp.float32)
    for k in range(4):
        base = lax.rem(scalars[20] + k, 4) * QUARTER
        rows = part[pl.ds(base, QUARTER)].reshape(QUARTER * TILE, TERMS * TILE)
        value = lax.dot_general(
            rows, right[...], (((1,), (1,)), ((), ())), preferred_element_type=jnp.float32
        ).reshape(QUARTER, TILE, TILE)
        outs[k][:, 0] = value.astype(jnp.bfloat16)
        bra = psi[pl.ds(base, QUARTER), 0, 0].astype(jnp.float32)
        numerator += jnp.sum(bra * value, 0)
        denominator += jnp.sum(bra * bra, 0)

    @pl.when(slot == 0)
    def _():
        sums[...] = jnp.zeros_like(sums)

    row = lax.broadcasted_iota(jnp.int32, (8, TILE), 0)
    live = (slot < scalars[21]).astype(jnp.float32)
    numerator = jnp.sum(numerator)
    denominator = jnp.sum(denominator) * (0.25 * live)
    sums[...] += jnp.where(row == 0, numerator, denominator)


def contract(scalars, mixed, left, psi, pieces):
    whole = lambda *shape: pl.BlockSpec(shape, lambda j, s: (0,) * len(shape))
    out = jax.ShapeDtypeStruct((QUARTER, SLOTS, TILE, TILE), jnp.bfloat16)
    return pl.pallas_call(
        kernel,
        grid_spec=pltpu.PrefetchScalarGridSpec(
            num_scalar_prefetch=1,
            grid=(SLOTS,),
            in_specs=[
                pl.BlockSpec((1, TERMS, PHYS, TILE, TILE), lambda j, s: (j, 0, 0, 0, 0)),
                whole(*left.shape),
                pl.BlockSpec((PHYS, 1, 1, TILE, TILE), lambda j, s: (0, 0, j, 0, 0)),
            ]
            + [whole(TERMS, TILE, TILE)] * 7,
            out_specs=[pl.BlockSpec((QUARTER, 1, TILE, TILE), lambda j, s: (0, j, 0, 0))] * 4
            + [whole(8, TILE)],
            scratch_shapes=[
                pltpu.VMEM((PHYS, TILE, TERMS * TILE), jnp.bfloat16),
                pltpu.VMEM((TILE, TERMS * TILE), jnp.bfloat16),
            ],
        ),
        out_shape=[out] * 4 + [jax.ShapeDtypeStruct((8, TILE), jnp.float32)],
        compiler_params=pltpu.CompilerParams(vmem_limit_bytes=48 << 20),
        cost_estimate=pl.CostEstimate(
            flops=4 * SLOTS * TERMS * PHYS * TILE**3, bytes_accessed=24 << 20, transcendentals=0
        ),
    )(scalars, mixed, left, psi, *pieces)


def body(psi, left_env, right_env, live_count, right_sector, pattern, term_op):
    group = lax.axis_index("mpo")
    blk = lax.axis_index("blk")
    own = lax.dynamic_slice_in_dim(right_env[0], group * TERMS, TERMS, 0)
    pieces = neighbours(own)
    live = jnp.arange(SLOTS, dtype=jnp.int32) < live_count[0]
    masked = jnp.where(live[None, None, :, None, None], psi, jnp.zeros_like(psi))
    mixed = jnp.stack(
        [
            jnp.einsum(
                "tpq,qab->tpab", term_op, masked[:, 0, j], preferred_element_type=jnp.float32
            ).astype(jnp.bfloat16)
            for j in range(SLOTS)
        ]
    )
    where = jnp.array(PIECE, jnp.int32)[blk % 2, right_sector[0] - blk + 3]
    scalars = jnp.concatenate(
        [pattern[:, 0], pattern[:, 1] - group * TERMS, where, group[None], live_count]
    ).astype(jnp.int32)
    o0, o1, o2, o3, sums = contract(scalars, mixed, left_env[0], psi, pieces)
    arrived = [shift(value, "mpo", d + 1) for d, value in enumerate((o1, o2, o3))]
    sums = total(sums)
    energy = sums[0, 0] / sums[1, 0]
    summed = functools.reduce(jnp.add, [a.astype(jnp.float32) for a in (o0, *arrived)])
    applied = summed.astype(jnp.bfloat16)
    ket = lax.dynamic_slice_in_dim(masked[:, 0], group * QUARTER, QUARTER, 0)
    residual = (applied.astype(jnp.float32) - energy * ket.astype(jnp.float32)).astype(jnp.bfloat16)
    return applied[:, None], residual[:, None], energy


def solution(mesh):
    placed = (
        P(None, "blk", None, None, None),
        P("blk", None, None, None),
        P("blk", None, None, None),
        P("blk"),
        P("blk", None),
        P("mpo", None),
        P("mpo", None, None),
    )
    return jax.shard_map(
        body,
        mesh=mesh,
        in_specs=placed,
        out_specs=(P("mpo", "blk", None, None, None), P("mpo", "blk", None, None, None), P()),
        check_vma=False,
    )
```

profile of v0, /device:TPU:1, one launch (start us, length us, event | category | flops | bytes accessed | tf_op | source)
XLA Modules:
  0.0 122.5 jit_solution(8408999530856696055)
XLA Ops:
  0.7 1.2 copy-done
  1.9 3.3 %collective-permute-start = (bf16[8,128,128]{2,1,0:T(8,128)(2,1)S(1)}, bf16[8,128,128]{2,1,0:T(8,128)(2,1)S(1)}, u32[]{:S(2)}, u32[]{:S(2)}) collective-permute-start(bf16[8,128,128]{2,1,0:T(8,128)(2,1)S(1)} %dynamic-slice_bitcast_fusion.p0), channel_id=1, source_target_pairs={{0,4},{4,0},{8,12},{12,8},{16,20},{20,16},{24,28},{28,24},{32,36},... | collective-permute-start | bytes 786440 | tf_op jit(solution)/shard_map/ppermute | solution.py:24
  5.2 6.0 %collective-permute-start.2 = (bf16[8,128,128]{2,1,0:T(8,128)(2,1)S(1)}, bf16[8,128,128]{2,1,0:T(8,128)(2,1)S(1)}, u32[]{:S(2)}, u32[]{:S(2)}) collective-permute-start(bf16[8,128,128]{2,1,0:T(8,128)(2,1)S(1)} %dynamic-slice_bitcast_fusion.p0), channel_id=1, source_target_pairs={{0,248},{4,252},{8,0},{12,4},{16,8},{20,12},{24,16},{28,20},{32,24... | collective-permute-start | bytes 786440 | tf_op jit(solution)/shard_map/ppermute | solution.py:20
  11.9 1.8 %bitcast_select_fusion = bf16[16,1,4,128,128]{4,3,2,0,1:T(8,128)(2,1)S(1)} fusion(bf16[16,1,4,128,128]{4,3,2,1,0:T(8,128)(2,1)} %psi.1, pred[4]{0:T(512)(128)(4,1)S(1)} %iota_compare_fusion), kind=kLoop, calls=%fused_computation.10 | loop fusion | flops 1048576 | bytes 4194308 | tf_op jit(solution)/shard_map/jit(_where)/select_n | solution.py:139
  14.0 1.0 copy-done.7
  15.0 1.2 %fusion.8 = bf16[128,128,8,16]{1,3,2,0:T(8,128)(2,1)S(1)} fusion(bf16[16,128,128,1]{2,1,0,3:T(8,128)(2,1)S(1)} %get-tuple-element.23, bf16[8,16,16]{2,1,0:T(8,128)(2,1)S(1)} %copy-done.8), kind=kOutput, calls=%fused_computation.21 | convolution fusion | flops 67108864 | bytes 4722688 | tf_op jit(solution)/shard_map/tpq,qab->tpab/dot_general | solution.py:142
  16.3 1.2 %fusion.6 = bf16[128,128,8,16]{1,3,2,0:T(8,128)(2,1)S(1)} fusion(bf16[16,128,128,1]{2,1,0,3:T(8,128)(2,1)S(1)} %get-tuple-element.22, bf16[8,16,16]{2,1,0:T(8,128)(2,1)S(1)} %copy-done.8), kind=kOutput, calls=%fused_computation.19 | convolution fusion | flops 67108864 | bytes 4722688 | tf_op jit(solution)/shard_map/tpq,qab->tpab/dot_general | solution.py:142
  17.5 1.2 %fusion.12 = bf16[128,128,8,16]{1,3,2,0:T(8,128)(2,1)S(1)} fusion(bf16[16,128,128,1]{2,1,0,3:T(8,128)(2,1)S(1)} %get-tuple-element.21, bf16[8,16,16]{2,1,0:T(8,128)(2,1)S(1)} %copy-done.8), kind=kOutput, calls=%fused_computation.25 | convolution fusion | flops 67108864 | bytes 4722688 | tf_op jit(solution)/shard_map/tpq,qab->tpab/dot_general | solution.py:142
  18.8 1.2 %fusion.10 = bf16[128,128,8,16]{1,3,2,0:T(8,128)(2,1)S(1)} fusion(bf16[16,128,128,1]{2,1,0,3:T(8,128)(2,1)S(1)} %get-tuple-element.24, bf16[8,16,16]{2,1,0:T(8,128)(2,1)S(1)} %copy-done.8), kind=kOutput, calls=%fused_computation.23 | convolution fusion | flops 67108864 | bytes 4722688 | tf_op jit(solution)/shard_map/tpq,qab->tpab/dot_general | solution.py:142
  20.0 7.2 %fusion.2 = (bf16[1,8,16,128,128]{4,3,2,1,0:T(8,128)(2,1)}, bf16[1,8,16,128,128]{4,3,2,1,0:T(8,128)(2,1)}) fusion(bf16[128,128,8,16]{1,3,2,0:T(8,128)(2,1)S(1)} %fusion.8, bf16[128,128,8,16]{1,3,2,0:T(8,128)(2,1)S(1)} %fusion.6), kind=kLoop, calls=%fused_computation.8 | loop fusion | bytes 16777216 | tf_op jit(solution)/shard_map/stack | solution.py:140
  27.2 7.1 %fusion = (bf16[1,8,16,128,128]{4,3,2,1,0:T(8,128)(2,1)}, bf16[1,8,16,128,128]{4,3,2,1,0:T(8,128)(2,1)}) fusion(bf16[128,128,8,16]{1,3,2,0:T(8,128)(2,1)S(1)} %fusion.12, bf16[128,128,8,16]{1,3,2,0:T(8,128)(2,1)S(1)} %fusion.10), kind=kLoop, calls=%fused_computation.6 | loop fusion | bytes 16777216 | tf_op jit(solution)/shard_map/stack | solution.py:140
  34.3 0.7 broadcast_select_fusion
  35.0 14.0 %pad_maximum_fusion.mixed = bf16[4,8,16,128,128]{4,3,2,1,0:T(8,128)(2,1)} fusion(bf16[1,8,16,128,128]{4,3,2,1,0:T(8,128)(2,1)} %get-tuple-element.32, bf16[1,8,16,128,128]{4,3,2,1,0:T(8,128)(2,1)} %get-tuple-element.31, bf16[1,8,16,128,128]{4,3,2,1,0:T(8,128)(2,1)} %get-tuple-element.30, bf16[1,8,16,128,128]{4,3,2,1,0:T(8,128)(2,1)} %get-tuple-element.29), kind=kLoop, calls=%fused_computation.1 | loop fusion | flops 25165824 | bytes 33554432 | tf_op jit(solution)/shard_map/stack | solution.py:140
  49.0 2.4 %collective-permute-start.3 = (bf16[8,128,128]{2,1,0:T(8,128)(2,1)S(1)}, bf16[8,128,128]{2,1,0:T(8,128)(2,1)S(1)}, u32[]{:S(2)}, u32[]{:S(2)}) collective-permute-start(bf16[8,128,128]{2,1,0:T(8,128)(2,1)S(1)} %collective-permute-done.1.p2), channel_id=1, source_target_pairs={{0,4},{4,0},{8,12},{12,8},{16,20},{20,16},{24,28},{28,24},{32,36},... | collective-permute-start | bytes 786440 | tf_op jit(solution)/shard_map/ppermute | solution.py:24
  52.7 0.7 copy-done.2
  54.1 0.9 copy-done.3
  55.1 0.9 copy-done.5
  56.0 15.6 %shard_map.103 = (bf16[4,4,128,128]{3,2,1,0:T(8,128)(2,1)S(1)}, bf16[4,4,128,128]{3,2,1,0:T(8,128)(2,1)}, bf16[4,4,128,128]{3,2,1,0:T(8,128)(2,1)}, bf16[4,4,128,128]{3,2,1,0:T(8,128)(2,1)}, f32[8,128]{1,0:T(8,128)S(1)}) custom-call(s32[22]{0:T(128)S(1)} %concatenate.7.scalars, bf16[4,8,16,128,128]{4,3,2,1,0:T(8,128)(2,1)} %pad_maximum_fusion.mixed, ...), custom_call_target="tpu_custom_call" | custom-call | flops 4294967296 | bytes 25165824 | tf_op jit(solution)/shard_map/pallas_call | solution.py:107
  71.7 1.1 collective-permute-done.10
  72.8 2.5 %collective-permute-done.11 = f32[8,128]{1,0:T(8,128)S(1)} collective-permute-done((f32[8,128]{1,0:T(8,128)S(1)}, f32[8,128]{1,0:T(8,128)S(1)}, u32[]{:S(2)}, u32[]{:S(2)}) %collective-permute-start.11) | collective-permute-done | bytes 4128 | tf_op jit(solution)/shard_map/ppermute | solution.py:42
  75.3 1.2 collective-permute-start.14
  76.4 1.0 collective-permute-start.13
  77.5 2.4 %collective-permute-start.12 = (f32[8,128]{1,0:T(8,128)S(1)}, f32[8,128]{1,0:T(8,128)S(1)}, u32[]{:S(2)}, u32[]{:S(2)}) collective-permute-start(f32[8,128]{1,0:T(8,128)S(1)} %add.100), channel_id=1, source_target_pairs={{0,64},{4,68},{8,72},{12,76},{16,80},{20,84},{24,88},{28,92},{32,9... | collective-permute-start | bytes 12296 | tf_op jit(solution)/shard_map/ppermute | solution.py:42
  79.8 3.0 %collective-permute-done.13 = f32[8,128]{1,0:T(8,128)S(1)} collective-permute-done((f32[8,128]{1,0:T(8,128)S(1)}, f32[8,128]{1,0:T(8,128)S(1)}, u32[]{:S(2)}, u32[]{:S(2)}) %collective-permute-start.13) | collective-permute-done | bytes 4128 | tf_op jit(solution)/shard_map/ppermute | solution.py:42
  82.8 3.8 %collective-permute-start.17 = (f32[8,128]{1,0:T(8,128)S(1)}, f32[8,128]{1,0:T(8,128)S(1)}, u32[]{:S(2)}, u32[]{:S(2)}) collective-permute-start(f32[8,128]{1,0:T(8,128)S(1)} %add_add_fusion.2), channel_id=1, source_target_pairs={{0,24},{4,28},{8,0},{12,4},{16,8},{20,12},{24,16},{28,20},{32,56},... | collective-permute-start | bytes 12296 | tf_op jit(solution)/shard_map/ppermute | solution.py:42
  87.3 2.7 %collective-permute-start.9 = (bf16[4,4,128,128]{3,2,1,0:T(8,128)(2,1)}, bf16[4,4,128,128]{3,2,1,0:T(8,128)(2,1)S(1)}, u32[]{:S(2)}, u32[]{:S(2)}) collective-permute-start(bf16[4,4,128,128]{3,2,1,0:T(8,128)(2,1)} %get-tuple-element.11), channel_id=1, source_target_pairs={{0,3},{1,0},{2,1},{3,2},{4,7},{5,4},{6,5},{7,6},{8,11},{9,8},{10,9... | collective-permute-start | bytes 1572872 | tf_op jit(solution)/shard_map/ppermute | solution.py:20
  91.1 2.3 %collective-permute-start.20 = (f32[8,128]{1,0:T(8,128)S(1)}, f32[8,128]{1,0:T(8,128)S(1)}, u32[]{:S(2)}, u32[]{:S(2)}) collective-permute-start(f32[8,128]{1,0:T(8,128)S(1)} %add_add_fusion.1), channel_id=1, source_target_pairs={{0,3},{1,0},{2,1},{3,2},{4,7},{5,4},{6,5},{7,6},{8,11},{9,8},{10,9... | collective-permute-start | bytes 12296 | tf_op jit(solution)/shard_map/ppermute | solution.py:20
  93.4 1.2 collective-permute-start.19
  94.6 14.5 %collective-permute-done.20 = f32[8,128]{1,0:T(8,128)S(1)} collective-permute-done((f32[8,128]{1,0:T(8,128)S(1)}, f32[8,128]{1,0:T(8,128)S(1)}, u32[]{:S(2)}, u32[]{:S(2)}) %collective-permute-start.20) | collective-permute-done | bytes 4128 | tf_op jit(solution)/shard_map/ppermute | solution.py:20
  109.1 3.7 %collective-permute-done.19 = f32[8,128]{1,0:T(8,128)S(1)} collective-permute-done((f32[8,128]{1,0:T(8,128)S(1)}, f32[8,128]{1,0:T(8,128)S(1)}, u32[]{:S(2)}, u32[]{:S(2)}) %collective-permute-start.19) | collective-permute-done | bytes 4128 | tf_op jit(solution)/shard_map/ppermute | solution.py:20
  112.8 4.2 %collective-permute-done.18 = f32[8,128]{1,0:T(8,128)S(1)} collective-permute-done((f32[8,128]{1,0:T(8,128)S(1)}, f32[8,128]{1,0:T(8,128)S(1)}, u32[]{:S(2)}, u32[]{:S(2)}) %collective-permute-start.18) | collective-permute-done | bytes 4128 | tf_op jit(solution)/shard_map/ppermute | solution.py:20
  118.9 2.5 %fusion.5 = (bf16[4,1,4,128,128]{4,3,2,1,0:T(8,128)(2,1)}, bf16[4,4,128,128]{3,2,1,0:T(8,128)(2,1)}) fusion(bf16[16,1,4,128,128]{4,3,2,0,1:T(8,128)(2,1)} %copy-done.7, s32[]{:T(128)S(6)} %select_n.47, f32[]{:T(128)} %bitcast.29, bf16[4,4,128,128]{3,2,1,0:T(8,128)(2,1)S(1)} %collective-permute-done.9, ...), kind=kLoop, calls=%fused_computation.14 | loop fusion | flops 3407872 | bytes 3670024
  (56 shorter events, 4.6 us)
Async XLA Ops:
  0.6 1.2 %copy-start = (bf16[1,32,128,128]{3,2,1,0:T(8,128)(2,1)S(1)}, bf16[1,32,128,128]{3,2,1,0:T(8,128)(2,1)}, u32[]{:S(2)}) copy-start(bf16[1,32,128,128]{3,2,1,0:T(8,128)(2,1)} %param.10) | copy-start | bytes 3145732
  1.9 50.8 %collective-permute-start = (bf16[8,128,128]{2,1,0:T(8,128)(2,1)S(1)}, bf16[8,128,128]{2,1,0:T(8,128)(2,1)S(1)}, u32[]{:S(2)}, u32[]{:S(2)}) collective-permute-start(bf16[8,128,128]{2,1,0:T(8,128)(2,1)S(1)} %dynamic-slice_bitcast_fusion.p0), channel_id=1, source_target_pairs={{0,4},{4,0},{8,12},{12,8},{16,20},{20,16},{24,28},{28,24},{32,36},... | collective-permute-start | bytes 786440 | tf_op jit(solution)/shard_map/ppermute | solution.py:24
  5.2 29.1 %collective-permute-start.1 = (bf16[8,128,128]{2,1,0:T(8,128)(2,1)S(1)}, bf16[8,128,128]{2,1,0:T(8,128)(2,1)S(1)}, u32[]{:S(2)}, u32[]{:S(2)}) collective-permute-start(bf16[8,128,128]{2,1,0:T(8,128)(2,1)S(1)} %dynamic-slice_bitcast_fusion.p0), channel_id=1, source_target_pairs={{0,8},{4,12},{8,16},{12,20},{16,24},{20,28},{24,32},{28,36},{32,40... | collective-permute-start | bytes 786440 | tf_op jit(solution)/shard_map/ppermute | solution.py:20
  5.2 29.1 %collective-permute-start.2 = (bf16[8,128,128]{2,1,0:T(8,128)(2,1)S(1)}, bf16[8,128,128]{2,1,0:T(8,128)(2,1)S(1)}, u32[]{:S(2)}, u32[]{:S(2)}) collective-permute-start(bf16[8,128,128]{2,1,0:T(8,128)(2,1)S(1)} %dynamic-slice_bitcast_fusion.p0), channel_id=1, source_target_pairs={{0,248},{4,252},{8,0},{12,4},{16,8},{20,12},{24,16},{28,20},{32,24... | collective-permute-start | bytes 786440 | tf_op jit(solution)/shard_map/ppermute | solution.py:20
  11.9 3.1 %copy-start.8 = (bf16[8,16,16]{2,1,0:T(8,128)(2,1)S(1)}, bf16[8,16,16]{2,1,0:T(8,128)(2,1)}, u32[]{:S(2)}) copy-start(bf16[8,16,16]{2,1,0:T(8,128)(2,1)} %param.14) | copy-start | bytes 12292
  13.7 1.3 %copy-start.7 = (bf16[16,1,4,128,128]{4,3,2,0,1:T(8,128)(2,1)}, bf16[16,1,4,128,128]{4,3,2,0,1:T(8,128)(2,1)S(1)}, u32[]{:S(2)}) copy-start(bf16[16,1,4,128,128]{4,3,2,0,1:T(8,128)(2,1)S(1)} %bitcast_select_fusion) | copy-start | bytes 6291460
  35.0 16.4 %collective-permute-start.5 = (bf16[8,128,128]{2,1,0:T(8,128)(2,1)}, bf16[8,128,128]{2,1,0:T(8,128)(2,1)}, u32[]{:S(2)}, u32[]{:S(2)}) collective-permute-start(bf16[8,128,128]{2,1,0:T(8,128)(2,1)} %broadcast_select_fusion), channel_id=1, source_target_pairs={{0,248},{4,12},{8,0},{12,20},{16,8},{20,28},{24,16},{28,36},{32,24... | collective-permute-start | bytes 786440 | tf_op jit(solution)/shard_map/ppermute | solution.py:34
  35.0 16.9 %copy-start.10 = (s32[1,4]{1,0:T(1,128)S(1)}, s32[1,4]{1,0:T(1,128)}, u32[]{:S(2)}) copy-start(s32[1,4]{1,0:T(1,128)} %param.12) | copy-start | bytes 52
  35.0 16.9 %copy-start.6 = (s32[2,7]{1,0:T(2,128)S(1)}, s32[2,7]{1,0:T(2,128)}, u32[]{:S(2)}) copy-start(s32[2,7]{1,0:T(2,128)} %constant.46.clone) | copy-start | bytes 172
  35.0 17.6 %copy-start.9 = (s32[8,2]{0,1:T(2,128)S(1)}, s32[8,2]{0,1:T(2,128)}, u32[]{:S(2)}) copy-start(s32[8,2]{0,1:T(2,128)} %param.13) | copy-start | bytes 196
  35.0 19.1 %copy-start.1 = (bf16[1,32,128,128]{3,2,1,0:T(8,128)(2,1)S(1)}, bf16[1,32,128,128]{3,2,1,0:T(8,128)(2,1)}, u32[]{:S(2)}) copy-start(bf16[1,32,128,128]{3,2,1,0:T(8,128)(2,1)} %param.9) | copy-start | bytes 3145732
  49.0 4.4 %collective-permute-start.3 = (bf16[8,128,128]{2,1,0:T(8,128)(2,1)S(1)}, bf16[8,128,128]{2,1,0:T(8,128)(2,1)S(1)}, u32[]{:S(2)}, u32[]{:S(2)}) collective-permute-start(bf16[8,128,128]{2,1,0:T(8,128)(2,1)S(1)} %collective-permute-done.1.p2), channel_id=1, source_target_pairs={{0,4},{4,0},{8,12},{12,8},{16,20},{20,16},{24,28},{28,24},{32,36},... | collective-permute-start | bytes 786440 | tf_op jit(solution)/shard_map/ppermute | solution.py:24
  51.4 2.7 %collective-permute-start.4 = (bf16[8,128,128]{2,1,0:T(8,128)(2,1)S(1)}, bf16[8,128,128]{2,1,0:T(8,128)(2,1)}, u32[]{:S(2)}, u32[]{:S(2)}) collective-permute-start(bf16[8,128,128]{2,1,0:T(8,128)(2,1)S(1)} %collective-permute-done.2.p3), channel_id=1, source_target_pairs={{0,4},{4,0},{8,12},{12,8},{16,20},{20,16},{24,28},{28,24},{32,36},... | collective-permute-start | bytes 786440 | tf_op jit(solution)/shard_map/ppermute | solution.py:24
  51.4 2.7 %collective-permute-start.6 = (bf16[8,128,128]{2,1,0:T(8,128)(2,1)}, bf16[8,128,128]{2,1,0:T(8,128)(2,1)}, u32[]{:S(2)}, u32[]{:S(2)}) collective-permute-start(bf16[8,128,128]{2,1,0:T(8,128)(2,1)} %collective-permute-done.5), channel_id=1, source_target_pairs={{0,4},{4,0},{8,12},{12,8},{16,20},{20,16},{24,28},{28,24},{32,36},... | collective-permute-start | bytes 786440 | tf_op jit(solution)/shard_map/ppermute | solution.py:24
  52.7 0.7 copy-start.2
  53.4 0.7 copy-start.4
  54.1 1.0 copy-start.3
  55.1 0.9 copy-start.5
  71.6 1.2 collective-permute-start.10
  72.8 2.5 %collective-permute-start.11 = (f32[8,128]{1,0:T(8,128)S(1)}, f32[8,128]{1,0:T(8,128)S(1)}, u32[]{:S(2)}, u32[]{:S(2)}) collective-permute-start(f32[8,128]{1,0:T(8,128)S(1)} %add.99), channel_id=1, source_target_pairs={{0,32},{4,36},{8,40},{12,44},{16,48},{20,52},{24,56},{28,60},{32,0... | collective-permute-start | bytes 12296 | tf_op jit(solution)/shard_map/ppermute | solution.py:42
  75.3 4.6 %collective-permute-start.14 = (f32[8,128]{1,0:T(8,128)S(1)}, f32[8,128]{1,0:T(8,128)S(1)}, u32[]{:S(2)}, u32[]{:S(2)}) collective-permute-start(f32[8,128]{1,0:T(8,128)S(1)} %add.100), channel_id=1, source_target_pairs={{0,192},{4,196},{8,200},{12,204},{16,208},{20,212},{24,216},{28,22... | collective-permute-start | bytes 12296 | tf_op jit(solution)/shard_map/ppermute | solution.py:42
  76.4 6.4 %collective-permute-start.13 = (f32[8,128]{1,0:T(8,128)S(1)}, f32[8,128]{1,0:T(8,128)S(1)}, u32[]{:S(2)}, u32[]{:S(2)}) collective-permute-start(f32[8,128]{1,0:T(8,128)S(1)} %add.100), channel_id=1, source_target_pairs={{0,128},{4,132},{8,136},{12,140},{16,144},{20,148},{24,152},{28,15... | collective-permute-start | bytes 12296 | tf_op jit(solution)/shard_map/ppermute | solution.py:42
  77.5 5.3 %collective-permute-start.12 = (f32[8,128]{1,0:T(8,128)S(1)}, f32[8,128]{1,0:T(8,128)S(1)}, u32[]{:S(2)}, u32[]{:S(2)}) collective-permute-start(f32[8,128]{1,0:T(8,128)S(1)} %add.100), channel_id=1, source_target_pairs={{0,64},{4,68},{8,72},{12,76},{16,80},{20,84},{24,88},{28,92},{32,9... | collective-permute-start | bytes 12296 | tf_op jit(solution)/shard_map/ppermute | solution.py:42
  82.8 7.6 %collective-permute-start.17 = (f32[8,128]{1,0:T(8,128)S(1)}, f32[8,128]{1,0:T(8,128)S(1)}, u32[]{:S(2)}, u32[]{:S(2)}) collective-permute-start(f32[8,128]{1,0:T(8,128)S(1)} %add_add_fusion.2), channel_id=1, source_target_pairs={{0,24},{4,28},{8,0},{12,4},{16,8},{20,12},{24,16},{28,20},{32,56},... | collective-permute-start | bytes 12296 | tf_op jit(solution)/shard_map/ppermute | solution.py:42
  86.6 4.4 %collective-permute-start.16 = (f32[8,128]{1,0:T(8,128)S(1)}, f32[8,128]{1,0:T(8,128)S(1)}, u32[]{:S(2)}, u32[]{:S(2)}) collective-permute-start(f32[8,128]{1,0:T(8,128)S(1)} %add_add_fusion.2), channel_id=1, source_target_pairs={{0,16},{4,20},{8,24},{12,28},{16,0},{20,4},{24,8},{28,12},{32,48},... | collective-permute-start | bytes 12296 | tf_op jit(solution)/shard_map/ppermute | solution.py:42
  86.6 4.4 %collective-permute-start.15 = (f32[8,128]{1,0:T(8,128)S(1)}, f32[8,128]{1,0:T(8,128)S(1)}, u32[]{:S(2)}, u32[]{:S(2)}) collective-permute-start(f32[8,128]{1,0:T(8,128)S(1)} %add_add_fusion.2), channel_id=1, source_target_pairs={{0,8},{4,12},{8,16},{12,20},{16,24},{20,28},{24,0},{28,4},{32,40},... | collective-permute-start | bytes 12296 | tf_op jit(solution)/shard_map/ppermute | solution.py:42
  87.3 31.6 %collective-permute-start.9 = (bf16[4,4,128,128]{3,2,1,0:T(8,128)(2,1)}, bf16[4,4,128,128]{3,2,1,0:T(8,128)(2,1)S(1)}, u32[]{:S(2)}, u32[]{:S(2)}) collective-permute-start(bf16[4,4,128,128]{3,2,1,0:T(8,128)(2,1)} %get-tuple-element.11), channel_id=1, source_target_pairs={{0,3},{1,0},{2,1},{3,2},{4,7},{5,4},{6,5},{7,6},{8,11},{9,8},{10,9... | collective-permute-start | bytes 1572872 | tf_op jit(solution)/shard_map/ppermute | solution.py:20
  90.0 28.8 %collective-permute-start.8 = (bf16[4,4,128,128]{3,2,1,0:T(8,128)(2,1)}, bf16[4,4,128,128]{3,2,1,0:T(8,128)(2,1)S(1)}, u32[]{:S(2)}, u32[]{:S(2)}) collective-permute-start(bf16[4,4,128,128]{3,2,1,0:T(8,128)(2,1)} %get-tuple-element.10), channel_id=1, source_target_pairs={{0,2},{1,3},{2,0},{3,1},{4,6},{5,7},{6,4},{7,5},{8,10},{9,11},{10,... | collective-permute-start | bytes 1572872 | tf_op jit(solution)/shard_map/ppermute | solution.py:20
  90.4 28.5 %collective-permute-start.7 = (bf16[4,4,128,128]{3,2,1,0:T(8,128)(2,1)}, bf16[4,4,128,128]{3,2,1,0:T(8,128)(2,1)S(1)}, u32[]{:S(2)}, u32[]{:S(2)}) collective-permute-start(bf16[4,4,128,128]{3,2,1,0:T(8,128)(2,1)} %get-tuple-element.9), channel_id=1, source_target_pairs={{0,1},{1,2},{2,3},{3,0},{4,5},{5,6},{6,7},{7,4},{8,9},{9,10},{10,1... | collective-permute-start | bytes 1572872 | tf_op jit(solution)/shard_map/ppermute | solution.py:20
  91.1 18.0 %collective-permute-start.20 = (f32[8,128]{1,0:T(8,128)S(1)}, f32[8,128]{1,0:T(8,128)S(1)}, u32[]{:S(2)}, u32[]{:S(2)}) collective-permute-start(f32[8,128]{1,0:T(8,128)S(1)} %add_add_fusion.1), channel_id=1, source_target_pairs={{0,3},{1,0},{2,1},{3,2},{4,7},{5,4},{6,5},{7,6},{8,11},{9,8},{10,9... | collective-permute-start | bytes 12296 | tf_op jit(solution)/shard_map/ppermute | solution.py:20
  93.4 19.4 %collective-permute-start.19 = (f32[8,128]{1,0:T(8,128)S(1)}, f32[8,128]{1,0:T(8,128)S(1)}, u32[]{:S(2)}, u32[]{:S(2)}) collective-permute-start(f32[8,128]{1,0:T(8,128)S(1)} %add_add_fusion.1), channel_id=1, source_target_pairs={{0,2},{1,3},{2,0},{3,1},{4,6},{5,7},{6,4},{7,5},{8,10},{9,11},{10,... | collective-permute-start | bytes 12296 | tf_op jit(solution)/shard_map/ppermute | solution.py:20
  109.1 7.8 %collective-permute-start.18 = (f32[8,128]{1,0:T(8,128)S(1)}, f32[8,128]{1,0:T(8,128)S(1)}, u32[]{:S(2)}, u32[]{:S(2)}) collective-permute-start(f32[8,128]{1,0:T(8,128)S(1)} %add_add_fusion.1), channel_id=1, source_target_pairs={{0,1},{1,2},{2,3},{3,0},{4,5},{5,6},{6,7},{7,4},{8,9},{9,10},{10,1... | collective-permute-start | bytes 12296 | tf_op jit(solution)/shard_map/ppermute | solution.py:20
where the time goes:
time: 124 us; the launch traced here: 122 us
  waiting for transfers between devices  29 us (23%)
  starting transfers between devices  28.6 us (23%)
  local copies, waits for them, and re-layouts  21.4 us (17%)
  other arithmetic  19 us (15%)
  Pallas kernels  15.6 us (13%)
  matrix products  4.94 us (4%)
  between operations  3.9 us (3%)
    ppermute x8, waiting for transfers between devices, shift(): lax.ppermute(value, axis, [(s, (s + steps) % count) for s in range(count)])  22.4 us
    pallas_call x1, Pallas kernels, contract(): pl.pallas_call(kernel, grid_spec=pltpu.PrefetchScalarGridSpec(num_scalar_...  15.6 us
    another operation x2, local copies, waits for them, and re-layouts, body(): jnp.stack([jnp.einsum('tpq,qab->tpab', term_op, masked[:, 0, j], preferre...  14.3 us
    another operation x1, other arithmetic, body(): jnp.stack([jnp.einsum('tpq,qab->tpab', term_op, masked[:, 0, j], preferre...  14 us
    ppermute x8, starting transfers between devices, shift(): lax.ppermute(value, axis, [(s, (s + steps) % count) for s in range(count)])  13.3 us
    ppermute x7, starting transfers between devices, ring(): lax.ppermute(value, 'blk', [(s, f(s)) for s in range(64)])  9.07 us
    ppermute x5, starting transfers between devices, swap(): lax.ppermute(value, 'blk', [(s, s ^ 1) for s in range(lax.axis_size('blk'...  6.24 us
    unnamed x22, local copies, waits for them, and re-layouts  5.58 us
  transfers between devices with their start and end apart: 21, of which 6 were waited for; matrix products, arithmetic and copies ran while one was open for 30% of the time, Pallas kernels for 0%

commit v1 on v0

v1 whole, which is shorter than its diff:
```python
import functools

import jax
import jax.numpy as jnp
from jax import lax
from jax.experimental import pallas as pl
from jax.experimental.pallas import tpu as pltpu
from jax.sharding import PartitionSpec as P

PIECE = ((6, 2, 4, 0, 1, 3, 5), (4, 2, 1, 0, 5, 3, 6))
TERMS = 8
PHYS = 16
SLOTS = 4
TILE = 128
QUARTER = 4
PAD = 136


def shift(value, axis, steps):
    count = lax.axis_size(axis)
    return lax.ppermute(value, axis, [(s, (s + steps) % count) for s in range(count)])


def swap(value):
    return lax.ppermute(value, "blk", [(s, s ^ 1) for s in range(lax.axis_size("blk"))])


def neighbours(own):
    count = lax.axis_size("blk")
    below = shift(own, "blk", 2)
    above = shift(own, "blk", -2)
    far = lax.ppermute(
        own, "blk", [(s, (s + 4) % count if s % 2 else (s - 4) % count) for s in range(count)]
    )
    return swap(own), below, above, far


def left_kernel(first, pattern, live_count, op, left, psi, after, part, token, ket, mixed):
    slot = pl.program_id(0)
    live = slot + first < live_count[0]
    for q in range(PHYS):
        image = psi[q, 0, 0].astype(jnp.float32)
        ket[q * PAD : q * PAD + TILE, :] = jnp.where(live, image, 0.0)
    for a in range(0, TILE, 4):
        columns = [ket[pl.ds(a + i, PHYS, stride=PAD), :].astype(jnp.bfloat16) for i in range(4)]
        product = jnp.dot(op[...], jnp.concatenate(columns, 1), preferred_element_type=jnp.float32)
        for i in range(4):
            mixed[pl.ds(a + i, TERMS * PHYS, stride=PAD), :] = product[:, i * TILE : (i + 1) * TILE]
    for t in range(TERMS):
        factor = left[pattern[t, 0]]
        for p in range(0, PHYS, 4):
            starts = [(t * PHYS + p + i) * PAD for i in range(4)]
            columns = [mixed[start : start + TILE].astype(jnp.bfloat16) for start in starts]
            product = jnp.dot(
                factor, jnp.concatenate(columns, 1), preferred_element_type=jnp.float32
            ).astype(jnp.bfloat16)
            for i in range(4):
                part[slot, p + i, :, t * TILE : (t + 1) * TILE] = product[:, i * TILE : (i + 1) * TILE]
    token[...] = mixed[:8, :]


def whole(*shape):
    return pl.BlockSpec(shape, lambda j, *s: (0,) * len(shape))


def in_hbm(value):
    return pltpu.with_memory_space_constraint(value, pltpu.HBM)


def in_vmem(value):
    return pltpu.with_memory_space_constraint(value, pltpu.VMEM)


def left_product(pattern, live_count, op, left, psi, after, first, count):
    return pl.pallas_call(
        functools.partial(left_kernel, first),
        grid_spec=pltpu.PrefetchScalarGridSpec(
            num_scalar_prefetch=2,
            grid=(count,),
            in_specs=[
                whole(*op.shape),
                whole(*left.shape),
                pl.BlockSpec((PHYS, 1, 1, TILE, TILE), lambda j, *s: (0, 0, j + first, 0, 0)),
                pl.BlockSpec(memory_space=pl.ANY),
            ],
            out_specs=[pl.BlockSpec(memory_space=pltpu.VMEM), whole(8, TILE)],
            scratch_shapes=[
                pltpu.VMEM((PHYS * PAD, TILE), jnp.float32),
                pltpu.VMEM((TERMS * PHYS * PAD, TILE), jnp.float32),
            ],
        ),
        out_shape=[
            pltpu.VMEM((count, PHYS, TILE, TERMS * TILE), jnp.bfloat16),
            jax.ShapeDtypeStruct((8, TILE), jnp.float32),
        ],
        compiler_params=pltpu.CompilerParams(vmem_limit_bytes=20 << 20),
        cost_estimate=pl.CostEstimate(
            flops=12 * count * TERMS * PHYS * TILE**3, bytes_accessed=count << 20, transcendentals=0
        ),
    )(pattern, live_count, op, in_hbm(left), in_hbm(psi), after)


def right_kernel(
    pattern, live_count, right_sector, part_a, part_b, psi, p0, p1, p2, p3, p4, p5, p6,
    o0, o1, o2, o3, ket, sums, right, total,
):
    slot = pl.program_id(0)
    group = lax.axis_index("mpo")
    blk = lax.axis_index("blk")
    pieces = (p0, p1, p2, p3, p4, p5, p6)
    outs = (o0, o1, o2, o3)
    distance = right_sector[0, slot] - blk
    which = jnp.int32(0)
    for d in range(7):
        piece = jnp.where(lax.rem(blk, 2) == 0, PIECE[0][d], PIECE[1][d])
        which = jnp.where(distance == d - 3, piece, which)
    for k in range(7):

        @pl.when(which == k)
        def _():
            for t in range(TERMS):
                right[t * TILE : (t + 1) * TILE, :] = pieces[k][pattern[t, 1] - group * TERMS].T

    @pl.when(slot == 0)
    def _():
        total[...] = jnp.zeros_like(total)

    live = slot < live_count[0]
    own = psi[pl.ds(group * QUARTER, QUARTER), 0, 0]
    ket[:, 0] = jnp.where(live, own, jnp.zeros_like(own))

    def block(part, index):
        numerator = jnp.zeros((TILE, TILE), jnp.float32)
        denominator = jnp.zeros((TILE, TILE), jnp.float32)
        for k in range(4):
            base = lax.rem(group + k, 4) * QUARTER
            rows = part[index, pl.ds(base, QUARTER)].reshape(QUARTER * TILE, TERMS * TILE)
            value = jnp.dot(rows, right[...], preferred_element_type=jnp.float32)
            value = value.reshape(QUARTER, TILE, TILE)
            outs[k][:, 0] = value.astype(jnp.bfloat16)
            bra = psi[pl.ds(base, QUARTER), 0, 0].astype(jnp.float32)
            numerator += jnp.sum(bra * value, 0)
            denominator += jnp.sum(bra * bra, 0)
        total[0] += numerator
        total[1] += denominator * jnp.where(live, 0.25, 0.0)

    split = part_a.shape[0]

    @pl.when(slot < split)
    def _():
        block(part_a, jnp.minimum(slot, split - 1))

    @pl.when(slot >= split)
    def _():
        block(part_b, jnp.maximum(slot - split, 0))

    @pl.when(slot == SLOTS - 1)
    def _():
        lane = lax.broadcasted_iota(jnp.int32, sums.shape, 2)
        sums[...] = jnp.where(lane < TILE // 2, jnp.sum(total[0]), jnp.sum(total[1]))


def right_product(pattern, live_count, right_sector, part_a, part_b, psi, pieces, devices):
    out = jax.ShapeDtypeStruct((QUARTER, SLOTS, TILE, TILE), jnp.bfloat16)
    resident = pl.BlockSpec(memory_space=pltpu.VMEM)
    return pl.pallas_call(
        right_kernel,
        grid_spec=pltpu.PrefetchScalarGridSpec(
            num_scalar_prefetch=3,
            grid=(SLOTS,),
            in_specs=[
                resident,
                resident,
                pl.BlockSpec((PHYS, 1, 1, TILE, TILE), lambda j, *s: (0, 0, j, 0, 0)),
            ]
            + [resident] * 7,
            out_specs=[pl.BlockSpec((QUARTER, 1, TILE, TILE), lambda j, *s: (0, j, 0, 0))] * 5
            + [whole(devices, 1, TILE)],
            scratch_shapes=[
                pltpu.VMEM((TERMS * TILE, TILE), jnp.bfloat16),
                pltpu.VMEM((2, TILE, TILE), jnp.float32),
            ],
        ),
        out_shape=[out] * 5 + [jax.ShapeDtypeStruct((devices, 1, TILE), jnp.float32)],
        compiler_params=pltpu.CompilerParams(vmem_limit_bytes=20 << 20),
        cost_estimate=pl.CostEstimate(
            flops=6 * SLOTS * TERMS * PHYS * TILE**3, bytes_accessed=5 << 20, transcendentals=0
        ),
    )(
        pattern, live_count, right_sector, in_vmem(part_a), in_vmem(part_b), in_hbm(psi),
        *map(in_vmem, pieces),
    )


def last_kernel(sums, o0, r1, r2, r3, ket, applied, residual, energy):
    first = pl.program_id(0) * 2
    lane = lax.broadcasted_iota(jnp.int32, (1, TILE), 1)
    value = jnp.sum(sums[...], 0)
    numerator = jnp.sum(jnp.where(lane == 0, value, 0.0), 1, keepdims=True)
    denominator = jnp.sum(jnp.where(lane == TILE // 2, value, 0.0), 1, keepdims=True)
    quotient = numerator / denominator
    for p in range(QUARTER):
        for j in range(2):
            result = sum(part[p, first + j].astype(jnp.float32) for part in (o0, r1, r2, r3))
            result = result.astype(jnp.bfloat16)
            applied[p, 0, j] = result
            rest = result.astype(jnp.float32) - quotient * ket[p, first + j].astype(jnp.float32)
            residual[p, 0, j] = rest.astype(jnp.bfloat16)
    energy[0, 0] = jnp.sum(quotient)


def last(sums, parts, ket):
    result = pl.BlockSpec((QUARTER, 1, 2, TILE, TILE), lambda j: (0, 0, j, 0, 0))
    out = jax.ShapeDtypeStruct((QUARTER, 1, SLOTS, TILE, TILE), jnp.bfloat16)
    return pl.pallas_call(
        last_kernel,
        grid=(SLOTS // 2,),
        in_specs=[pl.BlockSpec(memory_space=pltpu.VMEM)] * 6,
        out_specs=[result, result, pl.BlockSpec(memory_space=pltpu.SMEM)],
        out_shape=[out, out, jax.ShapeDtypeStruct((1, 1), jnp.float32)],
        compiler_params=pltpu.CompilerParams(vmem_limit_bytes=16 << 20),
        cost_estimate=pl.CostEstimate(flops=1 << 20, bytes_accessed=4 << 20, transcendentals=0),
    )(*map(in_vmem, (sums, *parts, ket)))


def body(psi, left_env, right_env, live_count, right_sector, pattern, term_op):
    group = lax.axis_index("mpo")
    op = term_op.reshape(TERMS * PHYS, PHYS)
    left = left_env[0]
    own = lax.dynamic_slice_in_dim(right_env[0], group * TERMS, TERMS, 0)
    other, below, above, far = neighbours(own)
    part_a, token = left_product(pattern, live_count, op, left, psi, live_count, 0, 3)
    token, below, above, far = lax.optimization_barrier((token, below, above, far))
    crossed = [swap(piece) for piece in (below, above, far)]
    part_b, _ = left_product(pattern, live_count, op, left, psi, token, 3, 1)
    pieces = (own, other, below, above, *crossed)
    devices = lax.axis_size("blk") * lax.axis_size("mpo")
    *parts, ket, sums = right_product(
        pattern, live_count, right_sector, part_a, part_b, psi, pieces, devices
    )
    arrived = [shift(value, "mpo", d + 1) for d, value in enumerate(parts[1:])]
    sums = lax.all_to_all(sums, ("blk", "mpo"), 0, 0, tiled=True)
    applied, residual, energy = last(sums, (parts[0], *arrived), ket)
    return applied, residual, energy[0, 0]


def solution(mesh):
    placed = (
        P(None, "blk", None, None, None),
        P("blk", None, None, None),
        P("blk", None, None, None),
        P("blk"),
        P("blk", None),
        P("mpo", None),
        P("mpo", None, None),
    )
    return jax.shard_map(
        body,
        mesh=mesh,
        in_specs=placed,
        out_specs=(P("mpo", "blk", None, None, None), P("mpo", "blk", None, None, None), P()),
        check_vma=False,
    )
```

time: 124 us -> 73.4 us (0.59)
  waiting for transfers between devices: 29 us -> 0.03 us
  blocking collectives: 0 us -> 24 us
  other arithmetic: 19 us -> 0 us
  local copies, waits for them, and re-layouts: 21.4 us -> 2.76 us
  Pallas kernels: 15.6 us -> 27.1 us
  starting transfers between devices: 28.6 us -> 17.7 us
  matrix products: 4.94 us -> 0 us
  between operations: 3.9 us -> 1.41 us
    all_to_all x0 -> x1, blocking collectives: none -> 24 us  [body(): sums = lax.all_to_all(sums, ('blk', 'mpo'), 0, 0, tiled=True)]
    ppermute x8 -> x5, waiting for transfers between devices: 22.4 us -> 0.01 us  [shift(): lax.ppermute(value, axis, [(s, (s + steps) % count) for s in range(count)])]
    another operation x2 -> x0, local copies, waits for them, and re-layouts: 14.3 us -> none  [body(): jnp.stack([jnp.einsum('tpq,qab->tpab', term_op, masked[:, 0, j], preferre...]
    another operation x1 -> x0, other arithmetic: 14 us -> none  [body(): jnp.stack([jnp.einsum('tpq,qab->tpab', term_op, masked[:, 0, j], preferre...]
    pallas_call x1 -> x4, Pallas kernels: 15.6 us -> 27.1 us  [the longest x2 17.1 us: left_product(): pl.pallas_call(functools.partial(left_kernel, first), grid_spec=pltpu.Pre...]
    ppermute x8 -> x1, starting transfers between devices: 9.07 us -> 1.01 us  [neighbours(): lax.ppermute(own, 'blk', [(s, (s + 4) % count if s % 2 else (s - 4) % cou...]
    ppermute x8 -> x1, waiting for transfers between devices: 5.42 us -> 0.01 us  [neighbours(): lax.ppermute(own, 'blk', [(s, (s + 4) % count if s % 2 else (s - 4) % cou...]
    dot_general x4 -> x0, matrix products: 4.94 us -> none  [body(): jnp.einsum('tpq,qab->tpab', term_op, masked[:, 0, j], preferred_element_t...]
  transfers between devices with their start and end apart: 21 -> 10, of which waited for: 6 -> 0; matrix products, arithmetic and copies ran while one was open for 30% -> 1% of each run, Pallas kernels for 0% -> 23%
where the time goes in v1:
time: 73.4 us; the launch traced here: 73.1 us
  Pallas kernels  27.1 us (37%)
  blocking collectives  24 us (33%)
  starting transfers between devices  17.7 us (24%)
  local copies, waits for them, and re-layouts  2.76 us (4%)
  between operations  1.41 us (2%)
    all_to_all x1, blocking collectives, body(): sums = lax.all_to_all(sums, ('blk', 'mpo'), 0, 0, tiled=True)  24 us
    pallas_call x2, Pallas kernels, left_product(): pl.pallas_call(functools.partial(left_kernel, first), grid_spec=pltpu.Pre...  17.1 us
    ppermute x5, starting transfers between devices, shift(): lax.ppermute(value, axis, [(s, (s + steps) % count) for s in range(count)])  10.1 us
    pallas_call x1, Pallas kernels, right_product(): pl.pallas_call(right_kernel, grid_spec=pltpu.PrefetchScalarGridSpec(num_s...  8.14 us
    ppermute x4, starting transfers between devices, swap(): lax.ppermute(value, 'blk', [(s, s ^ 1) for s in range(lax.axis_size('blk'...  6.58 us
    unnamed x7, local copies, waits for them, and re-layouts  2.74 us
    pallas_call x1, Pallas kernels, last(): pl.pallas_call(last_kernel, grid=(SLOTS // 2,), in_specs=[pl.BlockSpec(me...  1.87 us
  transfers between devices with their start and end apart: 10, of which 0 were waited for; matrix products, arithmetic and copies ran while one was open for 1% of the time, Pallas kernels for 23%

profile of v1, /device:TPU:1, one launch (start us, length us, event | category | flops | bytes accessed | tf_op | source)
XLA Modules:
  0.0 73.1 jit_solution(14375508516345321790)
XLA Ops:
  0.6 0.0 copy-start
  0.6 1.2 %copy-done = bf16[1,32,128,128]{3,2,1,0:T(8,128)(2,1)S(1)} copy-done((bf16[1,32,128,128]{3,2,1,0:T(8,128)(2,1)S(1)}, bf16[1,32,128,128]{3,2,1,0:T(8,128)(2,1)}, u32[]{:S(2)}) %copy-start) | copy-done | bytes 1048600
  1.9 3.3 %collective-permute-start.3 = (bf16[8,128,128]{2,1,0:T(8,128)(2,1)S(1)}, bf16[8,128,128]{2,1,0:T(8,128)(2,1)S(1)}, u32[]{:S(2)}, u32[]{:S(2)}) collective-permute-start(bf16[8,128,128]{2,1,0:T(8,128)(2,1)S(1)} %dynamic-slice_bitcast_fusion.p0), channel_id=1, source_target_pairs={{0,4},{4,0},{8,12},{12,8},{16,20},{20,16},{24,28},{28,24},{32,36},... | collective-permute-start | bytes 786440 | tf_op jit(solution)/shard_map/ppermute | solution.py:25
  5.2 1.0 %collective-permute-start.2 = (bf16[8,128,128]{2,1,0:T(8,128)(2,1)S(1)}, bf16[8,128,128]{2,1,0:T(8,128)(2,1)S(1)}, u32[]{:S(2)}, u32[]{:S(2)}) collective-permute-start(bf16[8,128,128]{2,1,0:T(8,128)(2,1)S(1)} %dynamic-slice_bitcast_fusion.p0), channel_id=1, source_target_pairs={{0,240},{4,20},{8,248},{12,28},{16,0},{20,36},{24,8},{28,44},{32,1... | collective-permute-start | bytes 786440 | tf_op jit(solution)/shard_map/ppermute | solution.py:32
  6.2 5.0 %collective-permute-start.1 = (bf16[8,128,128]{2,1,0:T(8,128)(2,1)S(1)}, bf16[8,128,128]{2,1,0:T(8,128)(2,1)S(1)}, u32[]{:S(2)}, u32[]{:S(2)}) collective-permute-start(bf16[8,128,128]{2,1,0:T(8,128)(2,1)S(1)} %dynamic-slice_bitcast_fusion.p0), channel_id=1, source_target_pairs={{0,248},{4,252},{8,0},{12,4},{16,8},{20,12},{24,16},{28,20},{32,24... | collective-permute-start | bytes 786440 | tf_op jit(solution)/shard_map/ppermute | solution.py:21
  11.2 0.0 collective-permute-start
  11.9 0.8 %copy.12.pattern = s32[8,2]{1,0:T(8,128)S(1)} copy(s32[8,2]{0,1:T(2,128)} %param.12) | data formatting | bytes 128 | tf_op args[5]
  12.7 0.0 copy-start.1
  12.7 0.8 %copy-done.1 = bf16[8,16,16]{2,1,0:T(8,128)(2,1)S(1)} copy-done((bf16[8,16,16]{2,1,0:T(8,128)(2,1)S(1)}, bf16[8,16,16]{2,1,0:T(8,128)(2,1)}, u32[]{:S(2)}) %copy-start.1) | copy-done | bytes 4120
  13.4 11.9 %shard_map.94 = (bf16[3,16,128,1024]{3,2,1,0:T(8,128)(2,1)S(1)}, f32[8,128]{1,0:T(8,128)S(1)}) custom-call(s32[8,2]{1,0:T(8,128)S(1)} %copy.12.pattern, s32[1]{0:T(128)S(6)} %copy.13.live_count.after, bf16[128,16]{1,0:T(8,128)(2,1)S(1)} %bitcast.5, bf16[32,128,128]{2,1,0:T(8,128)(2,1)} %bitcast.7, bf16[16,1,4,128,128]{4,3,2,1,0:T(8,128)(2,1)} %psi.5, ...), custom_call_target="tpu_custom_call" | custom-call | flops 9663676416 | bytes 3145728 | tf_op jit(solution)/shard_map/pallas_call | solution.py:75
  25.3 0.0 collective-permute-done.2
  25.3 0.0 collective-permute-done.1.p3
  25.3 0.0 collective-permute-done.p2
  25.3 0.0 copy-start.2
  25.4 2.7 %collective-permute-start.6 = (bf16[8,128,128]{2,1,0:T(8,128)(2,1)S(1)}, bf16[8,128,128]{2,1,0:T(8,128)(2,1)S(1)}, u32[]{:S(2)}, u32[]{:S(2)}) collective-permute-start(bf16[8,128,128]{2,1,0:T(8,128)(2,1)S(1)} %collective-permute-done.2), channel_id=1, source_target_pairs={{0,4},{4,0},{8,12},{12,8},{16,20},{20,16},{24,28},{28,24},{32,36},... | collective-permute-start | bytes 786440 | tf_op jit(solution)/shard_map/ppermute | solution.py:25
  28.1 0.1 collective-permute-start.4
  28.2 0.4 collective-permute-start.5
  28.6 5.2 %shard_map.95 = (bf16[1,16,128,1024]{3,2,1,0:T(8,128)(2,1)S(1)}, f32[8,128]{1,0:T(8,128)}) custom-call(s32[8,2]{1,0:T(8,128)S(1)} %copy.12.pattern, s32[1]{0:T(128)S(6)} %copy.13.live_count.after, bf16[128,16]{1,0:T(8,128)(2,1)S(1)} %bitcast.6, bf16[32,128,128]{2,1,0:T(8,128)(2,1)} %bitcast.8, bf16[16,1,4,128,128]{4,3,2,1,0:T(8,128)(2,1)} %psi.5, ...), custom_call_target="tpu_custom_call" | custom-call | flops 3221225472 | bytes 1048576 | tf_op jit(solution)/shard_map/pallas_call | solution.py:75
  33.9 0.0 collective-permute-done.3.p1
  33.9 0.0 collective-permute-done.6.p6
  33.9 0.0 collective-permute-done.4.p4
  33.9 0.0 collective-permute-done.5.p5
  33.9 0.0 copy-done.2
  33.9 8.1 %shard_map.96 = (bf16[4,4,128,128]{3,2,1,0:T(8,128)(2,1)S(1)}, bf16[4,4,128,128]{3,2,1,0:T(8,128)(2,1)S(1)}, bf16[4,4,128,128]{3,2,1,0:T(8,128)(2,1)S(1)}, bf16[...) custom-call(s32[8,2]{1,0:T(8,128)S(1)} %copy.12.pattern, ...), custom_call_target="tpu_custom_call" | custom-call | flops 6442450944 | bytes 5242880 | tf_op jit(solution)/shard_map/pallas_call | solution.py:166
  42.1 1.4 %collective-permute-start.7 = (bf16[4,4,128,128]{3,2,1,0:T(8,128)(2,1)S(1)}, bf16[4,4,128,128]{3,2,1,0:T(8,128)(2,1)S(1)}, u32[]{:S(2)}, u32[]{:S(2)}) collective-permute-start(bf16[4,4,128,128]{3,2,1,0:T(8,128)(2,1)S(1)} %get-tuple-element.28), channel_id=1, source_target_pairs={{0,1},{1,2},{2,3},{3,0},{4,5},{5,6},{6,7},{7,4},{8,9},{9,10},{10,1... | collective-permute-start | bytes 1572872 | tf_op jit(solution)/shard_map/ppermute | solution.py:21
  43.5 2.6 %collective-permute-start.8 = (bf16[4,4,128,128]{3,2,1,0:T(8,128)(2,1)S(1)}, bf16[4,4,128,128]{3,2,1,0:T(8,128)(2,1)S(1)}, u32[]{:S(2)}, u32[]{:S(2)}) collective-permute-start(bf16[4,4,128,128]{3,2,1,0:T(8,128)(2,1)S(1)} %get-tuple-element.29), channel_id=1, source_target_pairs={{0,2},{1,3},{2,0},{3,1},{4,6},{5,7},{6,4},{7,5},{8,10},{9,11},{10,... | collective-permute-start | bytes 1572872 | tf_op jit(solution)/shard_map/ppermute | solution.py:21
  46.1 1.1 %collective-permute-start.9 = (bf16[4,4,128,128]{3,2,1,0:T(8,128)(2,1)S(1)}, bf16[4,4,128,128]{3,2,1,0:T(8,128)(2,1)S(1)}, u32[]{:S(2)}, u32[]{:S(2)}) collective-permute-start(bf16[4,4,128,128]{3,2,1,0:T(8,128)(2,1)S(1)} %get-tuple-element.30), channel_id=1, source_target_pairs={{0,3},{1,0},{2,1},{3,2},{4,7},{5,4},{6,5},{7,6},{8,11},{9,8},{10,9... | collective-permute-start | bytes 1572872 | tf_op jit(solution)/shard_map/ppermute | solution.py:21
  47.2 24.0 %all_to_all.5.sums = f32[256,1,128]{2,1,0:T(1,128)S(1)} all-to-all(f32[256,1,128]{2,1,0:T(1,128)S(1)} %get-tuple-element.26), channel_id=1, replica_groups=mesh['blk'=64,'mpo'=4] {'blk','mpo'}, dimensions={0} | all-to-all | bytes 262144 | tf_op jit(solution)/shard_map/all_to_all | solution.py:242
  71.2 0.0 collective-permute-done.7.r1
  71.2 0.0 collective-permute-done.8.r2
  71.2 0.0 collective-permute-done.9.r3
  71.2 1.9 %shard_map.97 = (bf16[4,1,4,128,128]{4,3,2,1,0:T(8,128)(2,1)}, bf16[4,1,4,128,128]{4,3,2,1,0:T(8,128)(2,1)}, f32[1,1]{1,0:T(1,128)}) custom-call(f32[256,1,128]{2,1,0:T(1,128)S(1)} %all_to_all.5.sums, bf16[4,4,128,128]{3,2,1,0:T(8,128)(2,1)S(1)} %get-tuple-element.27.o0, bf16[4,4,128,128]{3,2,1,0:T(8,128)(2,1)S(1)} %collective-permute-done.7.r1, ...), custom_call_target="tpu_custom_call" | custom-call | flops 1048576 | bytes 4194304 | tf_op jit(solution)/shard_map/pallas_call | solution.py:215
  (1 shorter events, 0.0 us)
Async XLA Ops:
  0.6 1.2 %copy-start = (bf16[1,32,128,128]{3,2,1,0:T(8,128)(2,1)S(1)}, bf16[1,32,128,128]{3,2,1,0:T(8,128)(2,1)}, u32[]{:S(2)}) copy-start(bf16[1,32,128,128]{3,2,1,0:T(8,128)(2,1)} %param.9) | copy-start | bytes 3145732
  1.9 32.0 %collective-permute-start.3 = (bf16[8,128,128]{2,1,0:T(8,128)(2,1)S(1)}, bf16[8,128,128]{2,1,0:T(8,128)(2,1)S(1)}, u32[]{:S(2)}, u32[]{:S(2)}) collective-permute-start(bf16[8,128,128]{2,1,0:T(8,128)(2,1)S(1)} %dynamic-slice_bitcast_fusion.p0), channel_id=1, source_target_pairs={{0,4},{4,0},{8,12},{12,8},{16,20},{20,16},{24,28},{28,24},{32,36},... | collective-permute-start | bytes 786440 | tf_op jit(solution)/shard_map/ppermute | solution.py:25
  5.2 20.1 %collective-permute-start.2 = (bf16[8,128,128]{2,1,0:T(8,128)(2,1)S(1)}, bf16[8,128,128]{2,1,0:T(8,128)(2,1)S(1)}, u32[]{:S(2)}, u32[]{:S(2)}) collective-permute-start(bf16[8,128,128]{2,1,0:T(8,128)(2,1)S(1)} %dynamic-slice_bitcast_fusion.p0), channel_id=1, source_target_pairs={{0,240},{4,20},{8,248},{12,28},{16,0},{20,36},{24,8},{28,44},{32,1... | collective-permute-start | bytes 786440 | tf_op jit(solution)/shard_map/ppermute | solution.py:32
  6.2 19.1 %collective-permute-start.1 = (bf16[8,128,128]{2,1,0:T(8,128)(2,1)S(1)}, bf16[8,128,128]{2,1,0:T(8,128)(2,1)S(1)}, u32[]{:S(2)}, u32[]{:S(2)}) collective-permute-start(bf16[8,128,128]{2,1,0:T(8,128)(2,1)S(1)} %dynamic-slice_bitcast_fusion.p0), channel_id=1, source_target_pairs={{0,248},{4,252},{8,0},{12,4},{16,8},{20,12},{24,16},{28,20},{32,24... | collective-permute-start | bytes 786440 | tf_op jit(solution)/shard_map/ppermute | solution.py:21
  11.2 14.1 %collective-permute-start = (bf16[8,128,128]{2,1,0:T(8,128)(2,1)S(1)}, bf16[8,128,128]{2,1,0:T(8,128)(2,1)S(1)}, u32[]{:S(2)}, u32[]{:S(2)}) collective-permute-start(bf16[8,128,128]{2,1,0:T(8,128)(2,1)S(1)} %dynamic-slice_bitcast_fusion.p0), channel_id=1, source_target_pairs={{0,8},{4,12},{8,16},{12,20},{16,24},{20,28},{24,32},{28,36},{32,40... | collective-permute-start | bytes 786440 | tf_op jit(solution)/shard_map/ppermute | solution.py:21
  12.7 0.8 %copy-start.1 = (bf16[8,16,16]{2,1,0:T(8,128)(2,1)S(1)}, bf16[8,16,16]{2,1,0:T(8,128)(2,1)}, u32[]{:S(2)}) copy-start(bf16[8,16,16]{2,1,0:T(8,128)(2,1)} %param.13) | copy-start | bytes 12292
  25.3 8.6 %copy-start.2 = (s32[1,4]{1,0:T(1,128)S(1)}, s32[1,4]{1,0:T(1,128)}, u32[]{:S(2)}) copy-start(s32[1,4]{1,0:T(1,128)} %right_sector.1) | copy-start | bytes 52
  25.4 8.5 %collective-permute-start.6 = (bf16[8,128,128]{2,1,0:T(8,128)(2,1)S(1)}, bf16[8,128,128]{2,1,0:T(8,128)(2,1)S(1)}, u32[]{:S(2)}, u32[]{:S(2)}) collective-permute-start(bf16[8,128,128]{2,1,0:T(8,128)(2,1)S(1)} %collective-permute-done.2), channel_id=1, source_target_pairs={{0,4},{4,0},{8,12},{12,8},{16,20},{20,16},{24,28},{28,24},{32,36},... | collective-permute-start | bytes 786440 | tf_op jit(solution)/shard_map/ppermute | solution.py:25
  28.1 5.8 %collective-permute-start.4 = (bf16[8,128,128]{2,1,0:T(8,128)(2,1)S(1)}, bf16[8,128,128]{2,1,0:T(8,128)(2,1)S(1)}, u32[]{:S(2)}, u32[]{:S(2)}) collective-permute-start(bf16[8,128,128]{2,1,0:T(8,128)(2,1)S(1)} %collective-permute-done.p2), channel_id=1, source_target_pairs={{0,4},{4,0},{8,12},{12,8},{16,20},{20,16},{24,28},{28,24},{32,36},... | collective-permute-start | bytes 786440 | tf_op jit(solution)/shard_map/ppermute | solution.py:25
  28.2 5.7 %collective-permute-start.5 = (bf16[8,128,128]{2,1,0:T(8,128)(2,1)S(1)}, bf16[8,128,128]{2,1,0:T(8,128)(2,1)S(1)}, u32[]{:S(2)}, u32[]{:S(2)}) collective-permute-start(bf16[8,128,128]{2,1,0:T(8,128)(2,1)S(1)} %collective-permute-done.1.p3), channel_id=1, source_target_pairs={{0,4},{4,0},{8,12},{12,8},{16,20},{20,16},{24,28},{28,24},{32,36},... | collective-permute-start | bytes 786440 | tf_op jit(solution)/shard_map/ppermute | solution.py:25
  42.1 29.1 %collective-permute-start.7 = (bf16[4,4,128,128]{3,2,1,0:T(8,128)(2,1)S(1)}, bf16[4,4,128,128]{3,2,1,0:T(8,128)(2,1)S(1)}, u32[]{:S(2)}, u32[]{:S(2)}) collective-permute-start(bf16[4,4,128,128]{3,2,1,0:T(8,128)(2,1)S(1)} %get-tuple-element.28), channel_id=1, source_target_pairs={{0,1},{1,2},{2,3},{3,0},{4,5},{5,6},{6,7},{7,4},{8,9},{9,10},{10,1... | collective-permute-start | bytes 1572872 | tf_op jit(solution)/shard_map/ppermute | solution.py:21
  43.5 27.7 %collective-permute-start.8 = (bf16[4,4,128,128]{3,2,1,0:T(8,128)(2,1)S(1)}, bf16[4,4,128,128]{3,2,1,0:T(8,128)(2,1)S(1)}, u32[]{:S(2)}, u32[]{:S(2)}) collective-permute-start(bf16[4,4,128,128]{3,2,1,0:T(8,128)(2,1)S(1)} %get-tuple-element.29), channel_id=1, source_target_pairs={{0,2},{1,3},{2,0},{3,1},{4,6},{5,7},{6,4},{7,5},{8,10},{9,11},{10,... | collective-permute-start | bytes 1572872 | tf_op jit(solution)/shard_map/ppermute | solution.py:21
  46.1 25.1 %collective-permute-start.9 = (bf16[4,4,128,128]{3,2,1,0:T(8,128)(2,1)S(1)}, bf16[4,4,128,128]{3,2,1,0:T(8,128)(2,1)S(1)}, u32[]{:S(2)}, u32[]{:S(2)}) collective-permute-start(bf16[4,4,128,128]{3,2,1,0:T(8,128)(2,1)S(1)} %get-tuple-element.30), channel_id=1, source_target_pairs={{0,3},{1,0},{2,1},{3,2},{4,7},{5,4},{6,5},{7,6},{8,11},{9,8},{10,9... | collective-permute-start | bytes 1572872 | tf_op jit(solution)/shard_map/ppermute | solution.py:21

commit v2 on v1

v2 whole, which is shorter than its diff:
```python
import functools

import jax
import jax.numpy as jnp
from jax import lax
from jax.experimental import pallas as pl
from jax.experimental.pallas import tpu as pltpu
from jax.sharding import PartitionSpec as P

PIECE = (
    (6, 3, 5, 0, 1, 2, 4),
    (5, 3, 1, 0, 4, 2, 6),
    (6, 2, 4, 0, 1, 3, 5),
    (4, 2, 1, 0, 5, 3, 6),
)
TERMS = 8
PHYS = 16
SLOTS = 4
TILE = 128
QUARTER = 4


RESIDENT = pl.BlockSpec(memory_space=pltpu.VMEM)


def shift(value, axis, steps):
    count = lax.axis_size(axis)
    return lax.ppermute(value, axis, [(s, (s + steps) % count) for s in range(count)])


def trade(value, partner):
    count = lax.axis_size("blk")
    pairs = [(s, partner(s)) for s in range(count) if 0 <= partner(s) < count]
    return lax.ppermute(value, "blk", pairs)


def swap(value):
    return trade(value, lambda s: s ^ 1)


def passing_kernel(one, two, passed):
    place = lax.rem(lax.axis_index("blk"), 4)
    first = jnp.logical_or(place == 0, place == 3)

    @pl.when(first)
    def _():
        passed[...] = one[...]

    @pl.when(jnp.logical_not(first))
    def _():
        passed[...] = two[...]


def passing(one, two):
    return pl.pallas_call(
        passing_kernel,
        in_specs=[pl.BlockSpec(memory_space=pltpu.VMEM)] * 2,
        out_specs=pl.BlockSpec(memory_space=pltpu.VMEM),
        out_shape=pltpu.VMEM(one.shape, one.dtype),
        compiler_params=pltpu.CompilerParams(vmem_limit_bytes=1 << 20),
    )(in_vmem(one), in_vmem(two))


def whole(*shape):
    return pl.BlockSpec(shape, lambda j, *s: (0,) * len(shape))


def in_hbm(value):
    return pltpu.with_memory_space_constraint(value, pltpu.HBM)


def in_vmem(value):
    return pltpu.with_memory_space_constraint(value, pltpu.VMEM)


def own_kernel(environment, own, done):
    first = lax.axis_index("mpo") * TERMS
    copy = pltpu.make_async_copy(environment.at[0, pl.ds(first, TERMS)], own, done)
    copy.start()
    copy.wait()


def own_rows(environment):
    return pl.pallas_call(
        own_kernel,
        in_specs=[pl.BlockSpec(memory_space=pl.ANY)],
        out_specs=RESIDENT,
        out_shape=pltpu.VMEM((TERMS, TILE, TILE), jnp.bfloat16),
        scratch_shapes=[pltpu.SemaphoreType.DMA],
        compiler_params=pltpu.CompilerParams(vmem_limit_bytes=1 << 20),
    )(in_hbm(environment))


def spread(op, wide):
    rows, columns = wide.shape
    row = lax.broadcasted_iota(jnp.int32, (rows, TERMS * PHYS), 0)
    column = lax.broadcasted_iota(jnp.int32, (rows, TERMS * PHYS), 1)
    pick = (lax.div(row, PHYS) == column).astype(jnp.bfloat16)
    tall = jnp.dot(pick, op, preferred_element_type=jnp.float32).astype(jnp.bfloat16)
    row = lax.broadcasted_iota(jnp.int32, (PHYS, columns), 0)
    column = lax.broadcasted_iota(jnp.int32, (PHYS, columns), 1)
    pick = (lax.div(column, PHYS) == row).astype(jnp.bfloat16)
    full = jnp.dot(tall, pick, preferred_element_type=jnp.float32)
    row = lax.broadcasted_iota(jnp.int32, (rows, columns), 0)
    column = lax.broadcasted_iota(jnp.int32, (rows, columns), 1)
    same = lax.rem(row, PHYS) == lax.rem(column, PHYS)
    wide[...] = jnp.where(same, full, 0.0).astype(jnp.bfloat16)


def left_slot(live, pattern, wide, left, ready, psi, part, slot, mixed):
    for a in range(0, TILE, 32):
        halves = [psi[:, 0, 0, a + h : a + h + 16].reshape(PHYS * 16, TILE) for h in (0, 16)]
        columns = jnp.concatenate(halves, 1)
        columns = jnp.where(live, columns, jnp.zeros_like(columns))
        for m in range(0, TERMS * PHYS, 16):
            product = jnp.dot(
                wide[m * 16 : (m + 16) * 16], columns, preferred_element_type=jnp.float32
            ).astype(jnp.bfloat16)
            for h in (0, 1):
                half = product[:, h * TILE : (h + 1) * TILE].reshape(16, 16, TILE)
                mixed[m : m + 16, a + 16 * h : a + 16 * h + 16, :] = half
    ready()
    for t in range(TERMS):
        factor = left[pattern[0, t]]
        for p in range(0, PHYS, 4):
            columns = jnp.concatenate([mixed[t * PHYS + p + i] for i in range(4)], 1)
            product = jnp.dot(factor, columns, preferred_element_type=jnp.float32)
            product = product.astype(jnp.bfloat16)
            for i in range(4):
                part[slot, p + i, :, t * TILE : (t + 1) * TILE] = product[:, i * TILE : (i + 1) * TILE]


def left_first(pattern, live_count, op, left, psi, part, token, wide, kept, mixed, done):
    slot = pl.program_id(0)
    copy = pltpu.make_async_copy(left, kept, done)

    @pl.when(slot == 0)
    def _():
        copy.start()
        spread(op[...].reshape(TERMS * PHYS, PHYS), wide)
        token[...] = jnp.zeros_like(token)

    def ready():
        pl.when(slot == 0)(copy.wait)

    live = slot < live_count[0]
    left_slot(live, pattern, wide, kept, ready, psi, part, slot, mixed)


def left_second(first, pattern, live_count, wide, left, psi, before, part, mixed):
    slot = pl.program_id(0)
    live = slot + first < live_count[0]
    left_slot(live, pattern, wide, left, lambda: None, psi, part, slot, mixed)


def part_shape(count):
    return pltpu.VMEM((count, PHYS, TILE, TERMS * TILE), jnp.bfloat16)


def left_cost(count):
    return pl.CostEstimate(
        flops=12 * count * TERMS * PHYS * TILE**3, bytes_accessed=count << 20, transcendentals=0
    )


def left_early(pattern, live_count, op, left, psi, count):
    return pl.pallas_call(
        left_first,
        grid_spec=pltpu.PrefetchScalarGridSpec(
            num_scalar_prefetch=2,
            grid=(count,),
            in_specs=[
                whole(*op.shape),
                pl.BlockSpec(memory_space=pl.ANY),
                pl.BlockSpec((PHYS, 1, 1, TILE, TILE), lambda j, *s: (0, 0, j, 0, 0)),
            ],
            out_specs=[RESIDENT, whole(8, TILE), RESIDENT, RESIDENT],
            scratch_shapes=[
                pltpu.VMEM((TERMS * PHYS, TILE, TILE), jnp.bfloat16),
                pltpu.SemaphoreType.DMA,
            ],
        ),
        out_shape=[
            part_shape(count),
            jax.ShapeDtypeStruct((8, TILE), jnp.float32),
            pltpu.VMEM((TERMS * PHYS * 16, PHYS * 16), jnp.bfloat16),
            pltpu.VMEM(left.shape, jnp.bfloat16),
        ],
        compiler_params=pltpu.CompilerParams(vmem_limit_bytes=16 << 20),
        cost_estimate=left_cost(count),
    )(pattern, live_count, in_hbm(op), in_hbm(left), in_hbm(psi))


def left_late(pattern, live_count, wide, left, psi, before, first, count):
    return pl.pallas_call(
        functools.partial(left_second, first),
        grid_spec=pltpu.PrefetchScalarGridSpec(
            num_scalar_prefetch=2,
            grid=(count,),
            in_specs=[
                RESIDENT,
                RESIDENT,
                pl.BlockSpec((PHYS, 1, 1, TILE, TILE), lambda j, *s: (0, 0, j + first, 0, 0)),
                pl.BlockSpec(memory_space=pl.ANY),
            ],
            out_specs=RESIDENT,
            scratch_shapes=[pltpu.VMEM((TERMS * PHYS, TILE, TILE), jnp.bfloat16)],
        ),
        out_shape=part_shape(count),
        compiler_params=pltpu.CompilerParams(vmem_limit_bytes=16 << 20),
        cost_estimate=left_cost(count),
    )(pattern, live_count, in_vmem(wide), in_vmem(left), in_hbm(psi), before)


def right_kernel(
    pattern, live_count, right_sector, part_a, part_b, psi, p0, p1, p2, p3, p4, p5, p6,
    o0, o1, o2, o3, ket, sums, right, total,
):
    slot = pl.program_id(0)
    group = lax.axis_index("mpo")
    blk = lax.axis_index("blk")
    pieces = (p0, p1, p2, p3, p4, p5, p6)
    outs = (o0, o1, o2, o3)
    distance = right_sector[0, slot] - blk
    which = jnp.int32(0)
    for d in range(7):
        for r in range(4):
            here = jnp.logical_and(distance == d - 3, lax.rem(blk, 4) == r)
            which = jnp.where(here, PIECE[r][d], which)
    for k in range(7):

        @pl.when(which == k)
        def _():
            for t in range(TERMS):
                right[t * TILE : (t + 1) * TILE, :] = pieces[k][pattern[1, t] - group * TERMS].T

    @pl.when(slot == 0)
    def _():
        total[...] = jnp.zeros_like(total)

    live = slot < live_count[0]
    own = psi[pl.ds(group * QUARTER, QUARTER), 0, 0]
    ket[:, slot] = jnp.where(live, own, jnp.zeros_like(own))

    def block(part, index):
        numerator = jnp.zeros((TILE, TILE), jnp.float32)
        denominator = jnp.zeros((TILE, TILE), jnp.float32)
        for k in range(4):
            base = lax.rem(group + k, 4) * QUARTER
            rows = part[index, pl.ds(base, QUARTER)].reshape(QUARTER * TILE, TERMS * TILE)
            value = jnp.dot(rows, right[...], preferred_element_type=jnp.float32)
            value = value.reshape(QUARTER, TILE, TILE)
            outs[k][:, slot] = value.astype(jnp.bfloat16)
            bra = psi[pl.ds(base, QUARTER), 0, 0].astype(jnp.float32)
            numerator += jnp.sum(bra * value, 0)
            denominator += jnp.sum(bra * bra, 0)
        total[0] += numerator
        total[1] += denominator * jnp.where(live, 0.25, 0.0)

    split = part_a.shape[0]

    @pl.when(slot < split)
    def _():
        block(part_a, jnp.minimum(slot, split - 1))

    @pl.when(slot >= split)
    def _():
        block(part_b, jnp.maximum(slot - split, 0))

    @pl.when(slot == SLOTS - 1)
    def _():
        lane = lax.broadcasted_iota(jnp.int32, sums.shape, 2)
        sums[...] = jnp.where(lane < TILE // 2, jnp.sum(total[0]), jnp.sum(total[1]))


def right_product(pattern, live_count, right_sector, part_a, part_b, psi, pieces, devices):
    out = pltpu.VMEM((QUARTER, SLOTS, TILE, TILE), jnp.bfloat16)
    return pl.pallas_call(
        right_kernel,
        grid_spec=pltpu.PrefetchScalarGridSpec(
            num_scalar_prefetch=3,
            grid=(SLOTS,),
            in_specs=[
                RESIDENT,
                RESIDENT,
                pl.BlockSpec((PHYS, 1, 1, TILE, TILE), lambda j, *s: (0, 0, j, 0, 0)),
            ]
            + [RESIDENT] * 7,
            out_specs=[RESIDENT] * 6,
            scratch_shapes=[
                pltpu.VMEM((TERMS * TILE, TILE), jnp.bfloat16),
                pltpu.VMEM((2, TILE, TILE), jnp.float32),
            ],
        ),
        out_shape=[out] * 5 + [pltpu.VMEM((devices, 1, TILE), jnp.float32)],
        compiler_params=pltpu.CompilerParams(vmem_limit_bytes=12 << 20),
        cost_estimate=pl.CostEstimate(
            flops=6 * SLOTS * TERMS * PHYS * TILE**3, bytes_accessed=5 << 20, transcendentals=0
        ),
    )(
        pattern, live_count, right_sector, in_vmem(part_a), in_vmem(part_b), in_hbm(psi),
        *map(in_vmem, pieces),
    )


def last_kernel(sums, o0, r1, r2, r3, ket, applied, residual, energy):
    first = pl.program_id(0) * 2
    lane = lax.broadcasted_iota(jnp.int32, (1, TILE), 1)
    value = jnp.sum(sums[...], 0)
    numerator = jnp.sum(jnp.where(lane == 0, value, 0.0), 1, keepdims=True)
    denominator = jnp.sum(jnp.where(lane == TILE // 2, value, 0.0), 1, keepdims=True)
    quotient = numerator / denominator
    for p in range(QUARTER):
        for j in range(2):
            result = sum(part[p, first + j].astype(jnp.float32) for part in (o0, r1, r2, r3))
            result = result.astype(jnp.bfloat16)
            applied[p, 0, j] = result
            rest = result.astype(jnp.float32) - quotient * ket[p, first + j].astype(jnp.float32)
            residual[p, 0, j] = rest.astype(jnp.bfloat16)
    energy[0, 0] = jnp.sum(quotient)


def last(sums, parts, ket):
    result = pl.BlockSpec((QUARTER, 1, 2, TILE, TILE), lambda j: (0, 0, j, 0, 0))
    out = jax.ShapeDtypeStruct((QUARTER, 1, SLOTS, TILE, TILE), jnp.bfloat16)
    return pl.pallas_call(
        last_kernel,
        grid=(SLOTS // 2,),
        in_specs=[pl.BlockSpec(memory_space=pltpu.VMEM)] * 6,
        out_specs=[result, result, pl.BlockSpec(memory_space=pltpu.SMEM)],
        out_shape=[out, out, jax.ShapeDtypeStruct((1, 1), jnp.float32)],
        compiler_params=pltpu.CompilerParams(vmem_limit_bytes=16 << 20),
        cost_estimate=pl.CostEstimate(flops=1 << 20, bytes_accessed=4 << 20, transcendentals=0),
    )(*map(in_vmem, (sums, *parts, ket)))


def body(psi, left_env, right_env, live_count, right_sector, pattern, term_op):
    pattern = pattern.T
    own = own_rows(right_env)
    one = trade(own, lambda s: s ^ 2)
    two = trade(own, lambda s: s + 2 if s % 4 > 1 else s - 2)
    other = swap(own)
    part_a, token, wide, left = left_early(pattern, live_count, term_op, left_env[0], psi, 3)
    token, one, two = lax.optimization_barrier((token, one, two))
    far = trade(passing(one, two), lambda s: s + 1 if s % 2 else s - 1)
    pieces = (own, other, one, two, swap(one), swap(two), far)
    part_b = left_late(pattern, live_count, wide, left, psi, token, 3, 1)
    devices = lax.axis_size("blk") * lax.axis_size("mpo")
    *parts, ket, sums = right_product(
        pattern, live_count, right_sector, part_a, part_b, psi, pieces, devices
    )
    arrived = [shift(value, "mpo", d + 1) for d, value in enumerate(parts[1:])]
    sums = lax.all_to_all(sums, ("blk", "mpo"), 0, 0, tiled=True)
    applied, residual, energy = last(sums, (parts[0], *arrived), ket)
    return applied, residual, energy[0, 0]


def solution(mesh):
    placed = (
        P(None, "blk", None, None, None),
        P("blk", None, None, None),
        P("blk", None, None, None),
        P("blk"),
        P("blk", None),
        P("mpo", None),
        P("mpo", None, None),
    )
    return jax.shard_map(
        body,
        mesh=mesh,
        in_specs=placed,
        out_specs=(P("mpo", "blk", None, None, None), P("mpo", "blk", None, None, None), P()),
        check_vma=False,
    )
```

time: 73.4 us -> 69.7 us (0.950)
  starting transfers between devices: 17.7 us -> 13.8 us
  blocking collectives: 24 us -> 26.4 us
  local copies, waits for them, and re-layouts: 2.76 us -> 0.69 us
  waiting for transfers between devices: 0.03 us -> 1.46 us
  Pallas kernels: 27.1 us -> 25.7 us
    ppermute x5 -> x3, starting transfers between devices: 10.1 us -> 5.06 us  [shift(): lax.ppermute(value, axis, [(s, (s + steps) % count) for s in range(count)])]
    all_to_all x1, blocking collectives: 24 us -> 26.4 us  [body(): sums = lax.all_to_all(sums, ('blk', 'mpo'), 0, 0, tiled=True)]
    unnamed x7 -> x6, local copies, waits for them, and re-layouts: 2.74 us -> 0.69 us
    ppermute x5 -> x6, waiting for transfers between devices: 0.01 us -> 1.45 us  [trade(): return lax.ppermute(value, 'blk', pairs)]
    ppermute x5 -> x6, starting transfers between devices: 7.59 us -> 8.76 us  [trade(): return lax.ppermute(value, 'blk', pairs)]
    pallas_call x2 -> x4, Pallas kernels: 17.1 us -> 16 us  [the longest x1 10.8 us: left_early(): pl.pallas_call(left_first, grid_spec=pltpu.PrefetchScalarGridSpec(num_sca...]
  transfers between devices with their start and end apart: 10 -> 9, of which waited for: 0 -> 1; matrix products, arithmetic and copies ran while one was open for 1% -> 0% of each run, Pallas kernels for 23% -> 22%
where the time goes in v2:
time: 69.7 us; the launch traced here: 69.5 us
  blocking collectives  26.4 us (38%)
  Pallas kernels  25.7 us (37%)
  starting transfers between devices  13.8 us (20%)
  waiting for transfers between devices  1.46 us (2%)
  between operations  1.4 us (2%)
    all_to_all x1, blocking collectives, body(): sums = lax.all_to_all(sums, ('blk', 'mpo'), 0, 0, tiled=True)  26.4 us
    pallas_call x1, Pallas kernels, left_early(): pl.pallas_call(left_first, grid_spec=pltpu.PrefetchScalarGridSpec(num_sca...  10.8 us
    ppermute x6, starting transfers between devices, trade(): return lax.ppermute(value, 'blk', pairs)  8.76 us
    pallas_call x1, Pallas kernels, right_product(): pl.pallas_call(right_kernel, grid_spec=pltpu.PrefetchScalarGridSpec(num_s...  7.86 us
    ppermute x3, starting transfers between devices, shift(): lax.ppermute(value, axis, [(s, (s + steps) % count) for s in range(count)])  5.06 us
    pallas_call x1, Pallas kernels, left_late(): pl.pallas_call(functools.partial(left_second, first), grid_spec=pltpu.Pre...  4.2 us
    pallas_call x1, Pallas kernels, last(): pl.pallas_call(last_kernel, grid=(SLOTS // 2,), in_specs=[pl.BlockSpec(me...  1.87 us
    ppermute x6, waiting for transfers between devices, trade(): return lax.ppermute(value, 'blk', pairs)  1.45 us
  transfers between devices with their start and end apart: 9, of which 1 were waited for; matrix products, arithmetic and copies ran while one was open for 0% of the time, Pallas kernels for 22%

profile of v2, /device:TPU:1, one launch (start us, length us, event | category | flops | bytes accessed | tf_op | source)
XLA Modules:
  0.0 69.5 jit_solution(11699846930546399276)
XLA Ops:
  0.6 1.0 %shard_map.95.p0 = bf16[8,128,128]{2,1,0:T(8,128)(2,1)S(1)} custom-call(bf16[1,32,128,128]{3,2,1,0:T(8,128)(2,1)} %environment.1), custom_call_target="tpu_custom_call" | custom-call | tf_op jit(solution)/shard_map/pallas_call | solution.py:84
  1.6 3.3 %collective-permute-start.2 = (bf16[8,128,128]{2,1,0:T(8,128)(2,1)S(1)}, bf16[8,128,128]{2,1,0:T(8,128)(2,1)S(1)}, u32[]{:S(2)}, u32[]{:S(2)}) collective-permute-start(bf16[8,128,128]{2,1,0:T(8,128)(2,1)S(1)} %shard_map.95.p0), channel_id=1, source_target_pairs={{0,4},{4,0},{8,12},{12,8},{16,20},{20,16},{24,28},{28,24},{32,36},... | collective-permute-start | bytes 786440 | tf_op jit(solution)/shard_map/ppermute | solution.py:34
  4.9 0.7 collective-permute-start.1
  5.6 2.0 %collective-permute-start = (bf16[8,128,128]{2,1,0:T(8,128)(2,1)S(1)}, bf16[8,128,128]{2,1,0:T(8,128)(2,1)S(1)}, u32[]{:S(2)}, u32[]{:S(2)}) collective-permute-start(bf16[8,128,128]{2,1,0:T(8,128)(2,1)S(1)} %shard_map.95.p0), channel_id=1, source_target_pairs={{0,8},{4,12},{8,0},{12,4},{16,24},{20,28},{24,16},{28,20},{32,40},... | collective-permute-start | bytes 786440 | tf_op jit(solution)/shard_map/ppermute | solution.py:34
  8.3 0.0 copy-start
  8.3 0.7 copy-done
  8.9 10.8 %shard_map.94 = (bf16[3,16,128,1024]{3,2,1,0:T(8,128)(2,1)S(1)}, f32[8,128]{1,0:T(8,128)S(1)}, bf16[2048,256]{1,0:T(8,128)(2,1)S(1)}, bf16[32,128,128]{2,1,0:T(8,128)(2,1)S(1)}) custom-call(s32[2,8]{1,0:T(2,128)S(1)} %bitcast.3, s32[1]{0:T(128)S(6)} %copy.10.live_count, bf16[8,16,16]{2,1,0:T(8,128)(2,1)} %op.1, bf16[32,128,128]{2,1,0:T(8,128)(2,1)} %bitcast.6, ...), custom_call_target="tpu_custom_call" | custom-call | flops 9663676416 | bytes 3145728 | tf_op jit(solution)/shard_map/pallas_call | solution.py:167
  19.8 0.0 collective-permute-done.1.two.p3
  19.8 0.0 collective-permute-done.one.p2
  19.8 0.7 collective-permute-start.3
  20.5 0.1 collective-permute-start.4
  20.6 2.0 %collective-permute-start.5 = (bf16[8,128,128]{2,1,0:T(8,128)(2,1)S(1)}, bf16[8,128,128]{2,1,0:T(8,128)(2,1)S(1)}, u32[]{:S(2)}, u32[]{:S(2)}) collective-permute-start(bf16[8,128,128]{2,1,0:T(8,128)(2,1)S(1)} %shard_map.97), channel_id=1, source_target_pairs={{4,8},{8,4},{12,16},{16,12},{20,24},{24,20},{28,32},{32,28},{36,40... | collective-permute-start | bytes 786440 | tf_op jit(solution)/shard_map/ppermute | solution.py:34
  22.6 0.0 copy-start.1
  22.6 0.0 copy-start.2
  22.6 4.2 %shard_map.96.part_b = bf16[1,16,128,1024]{3,2,1,0:T(8,128)(2,1)S(1)} custom-call(s32[2,8]{1,0:T(2,128)S(1)} %bitcast.4, s32[1]{0:T(128)S(6)} %copy.10.live_count, bf16[2048,256]{1,0:T(8,128)(2,1)S(1)} %get-tuple-element.20.wide, bf16[32,128,128]{2,1,0:T(8,128)(2,1)S(1)} %get-tuple-element.21.left, bf16[16,1,4,128,128]{4,3,2,1,0:T(8,128)(2,1)} %psi.5, ...), custom_call_target="tpu_custom_call" | custom-call | flops 3221225472 | bytes 1048576 | tf_op jit(solution)/shard_map/pallas_call | solution.py:195
  26.8 0.0 collective-permute-done.2.p1
  26.8 1.4 %collective-permute-done.5.p6 = bf16[8,128,128]{2,1,0:T(8,128)(2,1)S(1)} collective-permute-done((bf16[8,128,128]{2,1,0:T(8,128)(2,1)S(1)}, bf16[8,128,128]{2,1,0:T(8,128)(2,1)S(1)}, u32[]{:S(2)}, u32[]{:S(2)}) %collective-permute-start.5) | collective-permute-done | bytes 262176 | tf_op jit(solution)/shard_map/ppermute | solution.py:34
  28.3 0.0 collective-permute-done.3.p4
  28.3 0.0 collective-permute-done.4.p5
  28.3 0.0 copy-done.1
  28.3 0.0 copy-done.2
  28.3 7.9 %shard_map.98 = (bf16[4,4,128,128]{3,2,1,0:T(8,128)(2,1)S(1)}, bf16[4,4,128,128]{3,2,1,0:T(8,128)(2,1)S(1)}, bf16[4,4,128,128]{3,2,1,0:T(8,128)(2,1)S(1)}, bf16[...) custom-call(s32[2,8]{1,0:T(2,128)S(1)} %bitcast.5, ...), custom_call_target="tpu_custom_call" | custom-call | flops 6442450944 | bytes 5242880 | tf_op jit(solution)/shard_map/pallas_call | solution.py:278
  36.2 1.4 %collective-permute-start.6 = (bf16[4,4,128,128]{3,2,1,0:T(8,128)(2,1)S(1)}, bf16[4,4,128,128]{3,2,1,0:T(8,128)(2,1)S(1)}, u32[]{:S(2)}, u32[]{:S(2)}) collective-permute-start(bf16[4,4,128,128]{3,2,1,0:T(8,128)(2,1)S(1)} %get-tuple-element.28), channel_id=1, source_target_pairs={{0,1},{1,2},{2,3},{3,0},{4,5},{5,6},{6,7},{7,4},{8,9},{9,10},{10,1... | collective-permute-start | bytes 1572872 | tf_op jit(solution)/shard_map/ppermute | solution.py:28
  37.5 2.6 %collective-permute-start.7 = (bf16[4,4,128,128]{3,2,1,0:T(8,128)(2,1)S(1)}, bf16[4,4,128,128]{3,2,1,0:T(8,128)(2,1)S(1)}, u32[]{:S(2)}, u32[]{:S(2)}) collective-permute-start(bf16[4,4,128,128]{3,2,1,0:T(8,128)(2,1)S(1)} %get-tuple-element.29), channel_id=1, source_target_pairs={{0,2},{1,3},{2,0},{3,1},{4,6},{5,7},{6,4},{7,5},{8,10},{9,11},{10,... | collective-permute-start | bytes 1572872 | tf_op jit(solution)/shard_map/ppermute | solution.py:28
  40.1 1.1 %collective-permute-start.8 = (bf16[4,4,128,128]{3,2,1,0:T(8,128)(2,1)S(1)}, bf16[4,4,128,128]{3,2,1,0:T(8,128)(2,1)S(1)}, u32[]{:S(2)}, u32[]{:S(2)}) collective-permute-start(bf16[4,4,128,128]{3,2,1,0:T(8,128)(2,1)S(1)} %get-tuple-element.30), channel_id=1, source_target_pairs={{0,3},{1,0},{2,1},{3,2},{4,7},{5,4},{6,5},{7,6},{8,11},{9,8},{10,9... | collective-permute-start | bytes 1572872 | tf_op jit(solution)/shard_map/ppermute | solution.py:28
  41.2 26.4 %all_to_all.5.sums = f32[256,1,128]{2,1,0:T(1,128)S(1)} all-to-all(f32[256,1,128]{2,1,0:T(1,128)S(1)} %get-tuple-element.26), channel_id=1, replica_groups=mesh['blk'=64,'mpo'=4] {'blk','mpo'}, dimensions={0} | all-to-all | bytes 262144 | tf_op jit(solution)/shard_map/all_to_all | solution.py:353
  67.6 0.0 collective-permute-done.6.r1
  67.6 0.0 collective-permute-done.7.r2
  67.6 0.0 collective-permute-done.8.r3
  67.6 1.9 %shard_map.99 = (bf16[4,1,4,128,128]{4,3,2,1,0:T(8,128)(2,1)}, bf16[4,1,4,128,128]{4,3,2,1,0:T(8,128)(2,1)}, f32[1,1]{1,0:T(1,128)}) custom-call(f32[256,1,128]{2,1,0:T(1,128)S(1)} %all_to_all.5.sums, bf16[4,4,128,128]{3,2,1,0:T(8,128)(2,1)S(1)} %get-tuple-element.27.o0, bf16[4,4,128,128]{3,2,1,0:T(8,128)(2,1)S(1)} %collective-permute-done.6.r1, ...), custom_call_target="tpu_custom_call" | custom-call | flops 1048576 | bytes 4194304 | tf_op jit(solution)/shard_map/pallas_call | solution.py:326
  (1 shorter events, 0.0 us)
Async XLA Ops:
  1.6 25.2 %collective-permute-start.2 = (bf16[8,128,128]{2,1,0:T(8,128)(2,1)S(1)}, bf16[8,128,128]{2,1,0:T(8,128)(2,1)S(1)}, u32[]{:S(2)}, u32[]{:S(2)}) collective-permute-start(bf16[8,128,128]{2,1,0:T(8,128)(2,1)S(1)} %shard_map.95.p0), channel_id=1, source_target_pairs={{0,4},{4,0},{8,12},{12,8},{16,20},{20,16},{24,28},{28,24},{32,36},... | collective-permute-start | bytes 786440 | tf_op jit(solution)/shard_map/ppermute | solution.py:34
  4.9 14.8 %collective-permute-start.1 = (bf16[8,128,128]{2,1,0:T(8,128)(2,1)S(1)}, bf16[8,128,128]{2,1,0:T(8,128)(2,1)S(1)}, u32[]{:S(2)}, u32[]{:S(2)}) collective-permute-start(bf16[8,128,128]{2,1,0:T(8,128)(2,1)S(1)} %shard_map.95.p0), channel_id=1, source_target_pairs={{8,16},{12,20},{16,8},{20,12},{24,32},{28,36},{32,24},{36,28},{40,... | collective-permute-start | bytes 786440 | tf_op jit(solution)/shard_map/ppermute | solution.py:34
  5.6 14.2 %collective-permute-start = (bf16[8,128,128]{2,1,0:T(8,128)(2,1)S(1)}, bf16[8,128,128]{2,1,0:T(8,128)(2,1)S(1)}, u32[]{:S(2)}, u32[]{:S(2)}) collective-permute-start(bf16[8,128,128]{2,1,0:T(8,128)(2,1)S(1)} %shard_map.95.p0), channel_id=1, source_target_pairs={{0,8},{4,12},{8,0},{12,4},{16,24},{20,28},{24,16},{28,20},{32,40},... | collective-permute-start | bytes 786440 | tf_op jit(solution)/shard_map/ppermute | solution.py:34
  8.3 0.7 copy-start
  19.8 8.5 %collective-permute-start.3 = (bf16[8,128,128]{2,1,0:T(8,128)(2,1)S(1)}, bf16[8,128,128]{2,1,0:T(8,128)(2,1)S(1)}, u32[]{:S(2)}, u32[]{:S(2)}) collective-permute-start(bf16[8,128,128]{2,1,0:T(8,128)(2,1)S(1)} %collective-permute-done.one.p2), channel_id=1, source_target_pairs={{0,4},{4,0},{8,12},{12,8},{16,20},{20,16},{24,28},{28,24},{32,36},... | collective-permute-start | bytes 786440 | tf_op jit(solution)/shard_map/ppermute | solution.py:34
  20.5 7.8 %collective-permute-start.4 = (bf16[8,128,128]{2,1,0:T(8,128)(2,1)S(1)}, bf16[8,128,128]{2,1,0:T(8,128)(2,1)S(1)}, u32[]{:S(2)}, u32[]{:S(2)}) collective-permute-start(bf16[8,128,128]{2,1,0:T(8,128)(2,1)S(1)} %collective-permute-done.1.two.p3), channel_id=1, source_target_pairs={{0,4},{4,0},{8,12},{12,8},{16,20},{20,16},{24,28},{28,24},{32,36},... | collective-permute-start | bytes 786440 | tf_op jit(solution)/shard_map/ppermute | solution.py:34
  20.6 7.7 %collective-permute-start.5 = (bf16[8,128,128]{2,1,0:T(8,128)(2,1)S(1)}, bf16[8,128,128]{2,1,0:T(8,128)(2,1)S(1)}, u32[]{:S(2)}, u32[]{:S(2)}) collective-permute-start(bf16[8,128,128]{2,1,0:T(8,128)(2,1)S(1)} %shard_map.97), channel_id=1, source_target_pairs={{4,8},{8,4},{12,16},{16,12},{20,24},{24,20},{28,32},{32,28},{36,40... | collective-permute-start | bytes 786440 | tf_op jit(solution)/shard_map/ppermute | solution.py:34
  22.6 5.7 %copy-start.1 = (s32[8,2]{0,1:T(2,128)S(1)}, s32[8,2]{0,1:T(2,128)}, u32[]{:S(2)}) copy-start(s32[8,2]{0,1:T(2,128)} %param.12) | copy-start | bytes 196
  22.6 5.7 %copy-start.2 = (s32[1,4]{1,0:T(1,128)S(1)}, s32[1,4]{1,0:T(1,128)}, u32[]{:S(2)}) copy-start(s32[1,4]{1,0:T(1,128)} %right_sector.1) | copy-start | bytes 52
  36.2 31.4 %collective-permute-start.6 = (bf16[4,4,128,128]{3,2,1,0:T(8,128)(2,1)S(1)}, bf16[4,4,128,128]{3,2,1,0:T(8,128)(2,1)S(1)}, u32[]{:S(2)}, u32[]{:S(2)}) collective-permute-start(bf16[4,4,128,128]{3,2,1,0:T(8,128)(2,1)S(1)} %get-tuple-element.28), channel_id=1, source_target_pairs={{0,1},{1,2},{2,3},{3,0},{4,5},{5,6},{6,7},{7,4},{8,9},{9,10},{10,1... | collective-permute-start | bytes 1572872 | tf_op jit(solution)/shard_map/ppermute | solution.py:28
  37.5 30.1 %collective-permute-start.7 = (bf16[4,4,128,128]{3,2,1,0:T(8,128)(2,1)S(1)}, bf16[4,4,128,128]{3,2,1,0:T(8,128)(2,1)S(1)}, u32[]{:S(2)}, u32[]{:S(2)}) collective-permute-start(bf16[4,4,128,128]{3,2,1,0:T(8,128)(2,1)S(1)} %get-tuple-element.29), channel_id=1, source_target_pairs={{0,2},{1,3},{2,0},{3,1},{4,6},{5,7},{6,4},{7,5},{8,10},{9,11},{10,... | collective-permute-start | bytes 1572872 | tf_op jit(solution)/shard_map/ppermute | solution.py:28
  40.1 27.5 %collective-permute-start.8 = (bf16[4,4,128,128]{3,2,1,0:T(8,128)(2,1)S(1)}, bf16[4,4,128,128]{3,2,1,0:T(8,128)(2,1)S(1)}, u32[]{:S(2)}, u32[]{:S(2)}) collective-permute-start(bf16[4,4,128,128]{3,2,1,0:T(8,128)(2,1)S(1)} %get-tuple-element.30), channel_id=1, source_target_pairs={{0,3},{1,0},{2,1},{3,2},{4,7},{5,4},{6,5},{7,6},{8,11},{9,8},{10,9... | collective-permute-start | bytes 1572872 | tf_op jit(solution)/shard_map/ppermute | solution.py:28

commit v3 on v2

--- a/solution.py
+++ b/solution.py
@@ -214,30 +214,43 @@
 
 def right_kernel(
     pattern, live_count, right_sector, part_a, part_b, psi, p0, p1, p2, p3, p4, p5, p6,
-    o0, o1, o2, o3, ket, sums, right, total,
+    o0, o1, o2, o3, ket, sums, chosen, right, total, done,
 ):
     slot = pl.program_id(0)
     group = lax.axis_index("mpo")
     blk = lax.axis_index("blk")
     pieces = (p0, p1, p2, p3, p4, p5, p6)
     outs = (o0, o1, o2, o3)
-    distance = right_sector[0, slot] - blk
-    which = jnp.int32(0)
-    for d in range(7):
-        for r in range(4):
-            here = jnp.logical_and(distance == d - 3, lax.rem(blk, 4) == r)
-            which = jnp.where(here, PIECE[r][d], which)
-    for k in range(7):
-
-        @pl.when(which == k)
-        def _():
-            for t in range(TERMS):
-                right[t * TILE : (t + 1) * TILE, :] = pieces[k][pattern[1, t] - group * TERMS].T
+
+    def choose(j):
+        distance = right_sector[0, j] - blk
+        which = jnp.int32(0)
+        for d in range(7):
+            for r in range(4):
+                here = jnp.logical_and(distance == d - 3, lax.rem(blk, 4) == r)
+                which = jnp.where(here, PIECE[r][d], which)
+        for k in range(7):
+            copy = pltpu.make_async_copy(pieces[k], chosen.at[j], done.at[j])
+            pl.when(which == k)(copy.start)
+
+    def arrive(j):
+        pltpu.make_async_copy(p0, chosen.at[j], done.at[j]).wait()
+
+    def turn(j):
+        for t in range(TERMS):
+            block = chosen[j, pattern[1, t] - group * TERMS]
+            right[lax.rem(j, 2), t * TILE : (t + 1) * TILE, :] = block.T
 
     @pl.when(slot == 0)
     def _():
+        for j in range(SLOTS):
+            choose(j)
         total[...] = jnp.zeros_like(total)
-
+        arrive(0)
+        turn(0)
+
+    following = jnp.minimum(slot + 1, SLOTS - 1)
+    pl.when(slot < SLOTS - 1)(lambda: arrive(following))
     live = slot < live_count[0]
     own = psi[pl.ds(group * QUARTER, QUARTER), 0, 0]
     ket[:, slot] = jnp.where(live, own, jnp.zeros_like(own))
@@ -248,7 +261,8 @@
         for k in range(4):
             base = lax.rem(group + k, 4) * QUARTER
             rows = part[index, pl.ds(base, QUARTER)].reshape(QUARTER * TILE, TERMS * TILE)
-            value = jnp.dot(rows, right[...], preferred_element_type=jnp.float32)
+            here = right[lax.rem(slot, 2)]
+            value = jnp.dot(rows, here, preferred_element_type=jnp.float32)
             value = value.reshape(QUARTER, TILE, TILE)
             outs[k][:, slot] = value.astype(jnp.bfloat16)
             bra = psi[pl.ds(base, QUARTER), 0, 0].astype(jnp.float32)
@@ -256,16 +270,11 @@
             denominator += jnp.sum(bra * bra, 0)
         total[0] += numerator
         total[1] += denominator * jnp.where(live, 0.25, 0.0)
+        turn(following)
 
     split = part_a.shape[0]
-
-    @pl.when(slot < split)
-    def _():
-        block(part_a, jnp.minimum(slot, split - 1))
-
-    @pl.when(slot >= split)
-    def _():
-        block(part_b, jnp.maximum(slot - split, 0))
+    pl.when(slot < split)(lambda: block(part_a, jnp.minimum(slot, split - 1)))
+    pl.when(slot >= split)(lambda: block(part_b, jnp.maximum(slot - split, 0)))
 
     @pl.when(slot == SLOTS - 1)
     def _():
@@ -288,8 +297,10 @@
             + [RESIDENT] * 7,
             out_specs=[RESIDENT] * 6,
             scratch_shapes=[
-                pltpu.VMEM((TERMS * TILE, TILE), jnp.bfloat16),
+                pltpu.VMEM((SLOTS, TERMS, TILE, TILE), jnp.bfloat16),
+                pltpu.VMEM((2, TERMS * TILE, TILE), jnp.bfloat16),
                 pltpu.VMEM((2, TILE, TILE), jnp.float32),
+                pltpu.SemaphoreType.DMA((SLOTS,)),
             ],
         ),
         out_shape=[out] * 5 + [pltpu.VMEM((devices, 1, TILE), jnp.float32)],
@@ -335,16 +346,16 @@
 
 
 def body(psi, left_env, right_env, live_count, right_sector, pattern, term_op):
-    pattern = pattern.T
+    pattern = in_hbm(pattern.T)
     own = own_rows(right_env)
     one = trade(own, lambda s: s ^ 2)
     two = trade(own, lambda s: s + 2 if s % 4 > 1 else s - 2)
     other = swap(own)
-    part_a, token, wide, left = left_early(pattern, live_count, term_op, left_env[0], psi, 3)
+    part_a, token, wide, left = left_early(pattern, live_count, term_op, left_env[0], psi, 2)
     token, one, two = lax.optimization_barrier((token, one, two))
     far = trade(passing(one, two), lambda s: s + 1 if s % 2 else s - 1)
     pieces = (own, other, one, two, swap(one), swap(two), far)
-    part_b = left_late(pattern, live_count, wide, left, psi, token, 3, 1)
+    part_b = left_late(pattern, live_count, wide, left, psi, token, 2, 2)
     devices = lax.axis_size("blk") * lax.axis_size("mpo")
     *parts, ket, sums = right_product(
         pattern, live_count, right_sector, part_a, part_b, psi, pieces, devices

time: 69.7 us -> 67.6 us (0.970)
  waiting for transfers between devices: 1.46 us -> 0.02 us
    pallas_call x1, Pallas kernels: 4.2 us -> 7.09 us  [left_late(): pl.pallas_call(functools.partial(left_second, first), grid_spec=pltpu.Pre...]
    pallas_call x1, Pallas kernels: 10.8 us -> 8.12 us  [left_early(): pl.pallas_call(left_first, grid_spec=pltpu.PrefetchScalarGridSpec(num_sca...]
    ppermute x6, waiting for transfers between devices: 1.45 us -> 0.02 us  [trade(): return lax.ppermute(value, 'blk', pairs)]
  transfers between devices with their start and end apart: 9 -> 9, of which waited for: 1 -> 0; matrix products, arithmetic and copies ran while one was open for 0% -> 0% of each run, Pallas kernels for 22% -> 23%
where the time goes in v3:
time: 67.6 us; the launch traced here: 67.1 us
  Pallas kernels  25.9 us (38%)
  blocking collectives  25.9 us (38%)
  starting transfers between devices  13.8 us (20%)
  between operations  1.41 us (2%)
    all_to_all x1, blocking collectives, body(): sums = lax.all_to_all(sums, ('blk', 'mpo'), 0, 0, tiled=True)  25.9 us
    ppermute x6, starting transfers between devices, trade(): return lax.ppermute(value, 'blk', pairs)  8.77 us
    pallas_call x1, Pallas kernels, left_early(): pl.pallas_call(left_first, grid_spec=pltpu.PrefetchScalarGridSpec(num_sca...  8.12 us
    pallas_call x1, Pallas kernels, right_product(): pl.pallas_call(right_kernel, grid_spec=pltpu.PrefetchScalarGridSpec(num_s...  7.82 us
    pallas_call x1, Pallas kernels, left_late(): pl.pallas_call(functools.partial(left_second, first), grid_spec=pltpu.Pre...  7.09 us
    ppermute x3, starting transfers between devices, shift(): lax.ppermute(value, axis, [(s, (s + steps) % count) for s in range(count)])  5.06 us
    pallas_call x1, Pallas kernels, last(): pl.pallas_call(last_kernel, grid=(SLOTS // 2,), in_specs=[pl.BlockSpec(me...  1.87 us
  transfers between devices with their start and end apart: 9, of which 0 were waited for; matrix products, arithmetic and copies ran while one was open for 0% of the time, Pallas kernels for 23%

profile of v3, /device:TPU:1, one launch (start us, length us, event | category | flops | bytes accessed | tf_op | source)
XLA Modules:
  0.0 67.1 jit_solution(16727989830846625557)
XLA Ops:
  0.6 1.0 %shard_map.95.p0 = bf16[8,128,128]{2,1,0:T(8,128)(2,1)S(1)} custom-call(bf16[1,32,128,128]{3,2,1,0:T(8,128)(2,1)} %environment.1), custom_call_target="tpu_custom_call" | custom-call | tf_op jit(solution)/shard_map/pallas_call | solution.py:84
  1.6 3.3 %collective-permute-start.2 = (bf16[8,128,128]{2,1,0:T(8,128)(2,1)S(1)}, bf16[8,128,128]{2,1,0:T(8,128)(2,1)S(1)}, u32[]{:S(2)}, u32[]{:S(2)}) collective-permute-start(bf16[8,128,128]{2,1,0:T(8,128)(2,1)S(1)} %shard_map.95.p0), channel_id=1, source_target_pairs={{0,4},{4,0},{8,12},{12,8},{16,20},{20,16},{24,28},{28,24},{32,36},... | collective-permute-start | bytes 786440 | tf_op jit(solution)/shard_map/ppermute | solution.py:34
  4.9 0.7 collective-permute-start.1
  5.6 2.0 %collective-permute-start = (bf16[8,128,128]{2,1,0:T(8,128)(2,1)S(1)}, bf16[8,128,128]{2,1,0:T(8,128)(2,1)S(1)}, u32[]{:S(2)}, u32[]{:S(2)}) collective-permute-start(bf16[8,128,128]{2,1,0:T(8,128)(2,1)S(1)} %shard_map.95.p0), channel_id=1, source_target_pairs={{0,8},{4,12},{8,0},{12,4},{16,24},{20,28},{24,16},{28,20},{32,40},... | collective-permute-start | bytes 786440 | tf_op jit(solution)/shard_map/ppermute | solution.py:34
  8.3 8.1 %shard_map.94 = (bf16[2,16,128,1024]{3,2,1,0:T(8,128)(2,1)S(1)}, f32[8,128]{1,0:T(8,128)S(1)}, bf16[2048,256]{1,0:T(8,128)(2,1)S(1)}, bf16[32,128,128]{2,1,0:T(8,128)(2,1)S(1)}) custom-call(s32[2,8]{1,0:T(2,128)} %bitcast.4, s32[1]{0:T(128)S(6)} %copy.10.live_count, bf16[8,16,16]{2,1,0:T(8,128)(2,1)} %op.1, bf16[32,128,128]{2,1,0:T(8,128)(2,1)} %bitcast.3, ...), custom_call_target="tpu_custom_call" | custom-call | flops 6442450944 | bytes 2097152 | tf_op jit(solution)/shard_map/pallas_call | solution.py:167
  16.4 0.0 collective-permute-done.1.two.p3
  16.4 0.0 collective-permute-done.one.p2
  16.4 0.7 %collective-permute-start.3 = (bf16[8,128,128]{2,1,0:T(8,128)(2,1)S(1)}, bf16[8,128,128]{2,1,0:T(8,128)(2,1)S(1)}, u32[]{:S(2)}, u32[]{:S(2)}) collective-permute-start(bf16[8,128,128]{2,1,0:T(8,128)(2,1)S(1)} %collective-permute-done.one.p2), channel_id=1, source_target_pairs={{0,4},{4,0},{8,12},{12,8},{16,20},{20,16},{24,28},{28,24},{32,36},... | collective-permute-start | bytes 786440 | tf_op jit(solution)/shard_map/ppermute | solution.py:34
  17.1 0.1 collective-permute-start.4
  17.2 2.0 %collective-permute-start.5 = (bf16[8,128,128]{2,1,0:T(8,128)(2,1)S(1)}, bf16[8,128,128]{2,1,0:T(8,128)(2,1)S(1)}, u32[]{:S(2)}, u32[]{:S(2)}) collective-permute-start(bf16[8,128,128]{2,1,0:T(8,128)(2,1)S(1)} %shard_map.97), channel_id=1, source_target_pairs={{4,8},{8,4},{12,16},{16,12},{20,24},{24,20},{28,32},{32,28},{36,40... | collective-permute-start | bytes 786440 | tf_op jit(solution)/shard_map/ppermute | solution.py:34
  19.2 0.0 copy-start
  19.2 7.1 %shard_map.96.part_b = bf16[2,16,128,1024]{3,2,1,0:T(8,128)(2,1)S(1)} custom-call(s32[2,8]{1,0:T(2,128)} %bitcast.5, s32[1]{0:T(128)S(6)} %copy.10.live_count, bf16[2048,256]{1,0:T(8,128)(2,1)S(1)} %get-tuple-element.20.wide, bf16[32,128,128]{2,1,0:T(8,128)(2,1)S(1)} %get-tuple-element.21.left, bf16[16,1,4,128,128]{4,3,2,1,0:T(8,128)(2,1)} %psi.5, ...), custom_call_target="tpu_custom_call" | custom-call | flops 6442450944 | bytes 2097152 | tf_op jit(solution)/shard_map/pallas_call | solution.py:195
  26.3 0.0 collective-permute-done.2.p1
  26.3 0.0 collective-permute-done.5.p6
  26.3 0.0 collective-permute-done.3.p4
  26.4 0.0 collective-permute-done.4.p5
  26.4 0.0 copy-done
  26.4 7.8 %shard_map.98 = (bf16[4,4,128,128]{3,2,1,0:T(8,128)(2,1)S(1)}, bf16[4,4,128,128]{3,2,1,0:T(8,128)(2,1)S(1)}, bf16[4,4,128,128]{3,2,1,0:T(8,128)(2,1)S(1)}, bf16[...) custom-call(s32[2,8]{1,0:T(2,128)} %bitcast.6, ...), custom_call_target="tpu_custom_call" | custom-call | flops 6442450944 | bytes 5242880 | tf_op jit(solution)/shard_map/pallas_call | solution.py:287
  34.2 1.4 %collective-permute-start.6 = (bf16[4,4,128,128]{3,2,1,0:T(8,128)(2,1)S(1)}, bf16[4,4,128,128]{3,2,1,0:T(8,128)(2,1)S(1)}, u32[]{:S(2)}, u32[]{:S(2)}) collective-permute-start(bf16[4,4,128,128]{3,2,1,0:T(8,128)(2,1)S(1)} %get-tuple-element.28), channel_id=1, source_target_pairs={{0,1},{1,2},{2,3},{3,0},{4,5},{5,6},{6,7},{7,4},{8,9},{9,10},{10,1... | collective-permute-start | bytes 1572872 | tf_op jit(solution)/shard_map/ppermute | solution.py:28
  35.6 2.6 %collective-permute-start.7 = (bf16[4,4,128,128]{3,2,1,0:T(8,128)(2,1)S(1)}, bf16[4,4,128,128]{3,2,1,0:T(8,128)(2,1)S(1)}, u32[]{:S(2)}, u32[]{:S(2)}) collective-permute-start(bf16[4,4,128,128]{3,2,1,0:T(8,128)(2,1)S(1)} %get-tuple-element.29), channel_id=1, source_target_pairs={{0,2},{1,3},{2,0},{3,1},{4,6},{5,7},{6,4},{7,5},{8,10},{9,11},{10,... | collective-permute-start | bytes 1572872 | tf_op jit(solution)/shard_map/ppermute | solution.py:28
  38.2 1.1 %collective-permute-start.8 = (bf16[4,4,128,128]{3,2,1,0:T(8,128)(2,1)S(1)}, bf16[4,4,128,128]{3,2,1,0:T(8,128)(2,1)S(1)}, u32[]{:S(2)}, u32[]{:S(2)}) collective-permute-start(bf16[4,4,128,128]{3,2,1,0:T(8,128)(2,1)S(1)} %get-tuple-element.30), channel_id=1, source_target_pairs={{0,3},{1,0},{2,1},{3,2},{4,7},{5,4},{6,5},{7,6},{8,11},{9,8},{10,9... | collective-permute-start | bytes 1572872 | tf_op jit(solution)/shard_map/ppermute | solution.py:28
  39.3 25.9 %all_to_all.5.sums = f32[256,1,128]{2,1,0:T(1,128)S(1)} all-to-all(f32[256,1,128]{2,1,0:T(1,128)S(1)} %get-tuple-element.26), channel_id=1, replica_groups=mesh['blk'=64,'mpo'=4] {'blk','mpo'}, dimensions={0} | all-to-all | bytes 262144 | tf_op jit(solution)/shard_map/all_to_all | solution.py:364
  65.2 0.0 collective-permute-done.6.r1
  65.2 0.0 collective-permute-done.7.r2
  65.2 0.0 collective-permute-done.8.r3
  65.2 1.9 %shard_map.99 = (bf16[4,1,4,128,128]{4,3,2,1,0:T(8,128)(2,1)}, bf16[4,1,4,128,128]{4,3,2,1,0:T(8,128)(2,1)}, f32[1,1]{1,0:T(1,128)}) custom-call(f32[256,1,128]{2,1,0:T(1,128)S(1)} %all_to_all.5.sums, bf16[4,4,128,128]{3,2,1,0:T(8,128)(2,1)S(1)} %get-tuple-element.27.o0, bf16[4,4,128,128]{3,2,1,0:T(8,128)(2,1)S(1)} %collective-permute-done.6.r1, ...), custom_call_target="tpu_custom_call" | custom-call | flops 1048576 | bytes 4194304 | tf_op jit(solution)/shard_map/pallas_call | solution.py:337
  (1 shorter events, 0.0 us)
Async XLA Ops:
  1.6 24.7 %collective-permute-start.2 = (bf16[8,128,128]{2,1,0:T(8,128)(2,1)S(1)}, bf16[8,128,128]{2,1,0:T(8,128)(2,1)S(1)}, u32[]{:S(2)}, u32[]{:S(2)}) collective-permute-start(bf16[8,128,128]{2,1,0:T(8,128)(2,1)S(1)} %shard_map.95.p0), channel_id=1, source_target_pairs={{0,4},{4,0},{8,12},{12,8},{16,20},{20,16},{24,28},{28,24},{32,36},... | collective-permute-start | bytes 786440 | tf_op jit(solution)/shard_map/ppermute | solution.py:34
  4.9 11.5 %collective-permute-start.1 = (bf16[8,128,128]{2,1,0:T(8,128)(2,1)S(1)}, bf16[8,128,128]{2,1,0:T(8,128)(2,1)S(1)}, u32[]{:S(2)}, u32[]{:S(2)}) collective-permute-start(bf16[8,128,128]{2,1,0:T(8,128)(2,1)S(1)} %shard_map.95.p0), channel_id=1, source_target_pairs={{8,16},{12,20},{16,8},{20,12},{24,32},{28,36},{32,24},{36,28},{40,... | collective-permute-start | bytes 786440 | tf_op jit(solution)/shard_map/ppermute | solution.py:34
  5.6 10.8 %collective-permute-start = (bf16[8,128,128]{2,1,0:T(8,128)(2,1)S(1)}, bf16[8,128,128]{2,1,0:T(8,128)(2,1)S(1)}, u32[]{:S(2)}, u32[]{:S(2)}) collective-permute-start(bf16[8,128,128]{2,1,0:T(8,128)(2,1)S(1)} %shard_map.95.p0), channel_id=1, source_target_pairs={{0,8},{4,12},{8,0},{12,4},{16,24},{20,28},{24,16},{28,20},{32,40},... | collective-permute-start | bytes 786440 | tf_op jit(solution)/shard_map/ppermute | solution.py:34
  16.4 9.9 %collective-permute-start.3 = (bf16[8,128,128]{2,1,0:T(8,128)(2,1)S(1)}, bf16[8,128,128]{2,1,0:T(8,128)(2,1)S(1)}, u32[]{:S(2)}, u32[]{:S(2)}) collective-permute-start(bf16[8,128,128]{2,1,0:T(8,128)(2,1)S(1)} %collective-permute-done.one.p2), channel_id=1, source_target_pairs={{0,4},{4,0},{8,12},{12,8},{16,20},{20,16},{24,28},{28,24},{32,36},... | collective-permute-start | bytes 786440 | tf_op jit(solution)/shard_map/ppermute | solution.py:34
  17.1 9.3 %collective-permute-start.4 = (bf16[8,128,128]{2,1,0:T(8,128)(2,1)S(1)}, bf16[8,128,128]{2,1,0:T(8,128)(2,1)S(1)}, u32[]{:S(2)}, u32[]{:S(2)}) collective-permute-start(bf16[8,128,128]{2,1,0:T(8,128)(2,1)S(1)} %collective-permute-done.1.two.p3), channel_id=1, source_target_pairs={{0,4},{4,0},{8,12},{12,8},{16,20},{20,16},{24,28},{28,24},{32,36},... | collective-permute-start | bytes 786440 | tf_op jit(solution)/shard_map/ppermute | solution.py:34
  17.2 9.1 %collective-permute-start.5 = (bf16[8,128,128]{2,1,0:T(8,128)(2,1)S(1)}, bf16[8,128,128]{2,1,0:T(8,128)(2,1)S(1)}, u32[]{:S(2)}, u32[]{:S(2)}) collective-permute-start(bf16[8,128,128]{2,1,0:T(8,128)(2,1)S(1)} %shard_map.97), channel_id=1, source_target_pairs={{4,8},{8,4},{12,16},{16,12},{20,24},{24,20},{28,32},{32,28},{36,40... | collective-permute-start | bytes 786440 | tf_op jit(solution)/shard_map/ppermute | solution.py:34
  19.2 7.2 %copy-start = (s32[1,4]{1,0:T(1,128)S(1)}, s32[1,4]{1,0:T(1,128)}, u32[]{:S(2)}) copy-start(s32[1,4]{1,0:T(1,128)} %right_sector.1) | copy-start | bytes 52
  34.2 31.0 %collective-permute-start.6 = (bf16[4,4,128,128]{3,2,1,0:T(8,128)(2,1)S(1)}, bf16[4,4,128,128]{3,2,1,0:T(8,128)(2,1)S(1)}, u32[]{:S(2)}, u32[]{:S(2)}) collective-permute-start(bf16[4,4,128,128]{3,2,1,0:T(8,128)(2,1)S(1)} %get-tuple-element.28), channel_id=1, source_target_pairs={{0,1},{1,2},{2,3},{3,0},{4,5},{5,6},{6,7},{7,4},{8,9},{9,10},{10,1... | collective-permute-start | bytes 1572872 | tf_op jit(solution)/shard_map/ppermute | solution.py:28
  35.6 29.6 %collective-permute-start.7 = (bf16[4,4,128,128]{3,2,1,0:T(8,128)(2,1)S(1)}, bf16[4,4,128,128]{3,2,1,0:T(8,128)(2,1)S(1)}, u32[]{:S(2)}, u32[]{:S(2)}) collective-permute-start(bf16[4,4,128,128]{3,2,1,0:T(8,128)(2,1)S(1)} %get-tuple-element.29), channel_id=1, source_target_pairs={{0,2},{1,3},{2,0},{3,1},{4,6},{5,7},{6,4},{7,5},{8,10},{9,11},{10,... | collective-permute-start | bytes 1572872 | tf_op jit(solution)/shard_map/ppermute | solution.py:28
  38.2 27.0 %collective-permute-start.8 = (bf16[4,4,128,128]{3,2,1,0:T(8,128)(2,1)S(1)}, bf16[4,4,128,128]{3,2,1,0:T(8,128)(2,1)S(1)}, u32[]{:S(2)}, u32[]{:S(2)}) collective-permute-start(bf16[4,4,128,128]{3,2,1,0:T(8,128)(2,1)S(1)} %get-tuple-element.30), channel_id=1, source_target_pairs={{0,3},{1,0},{2,1},{3,2},{4,7},{5,4},{6,5},{7,6},{8,11},{9,8},{10,9... | collective-permute-start | bytes 1572872 | tf_op jit(solution)/shard_map/ppermute | solution.py:28

commit v4 on v3

--- a/solution.py
+++ b/solution.py
@@ -107,11 +107,10 @@
     wide[...] = jnp.where(same, full, 0.0).astype(jnp.bfloat16)
 
 
-def left_slot(live, pattern, wide, left, ready, psi, part, slot, mixed):
+def left_slot(pattern, wide, left, ready, psi, part, slot, mixed):
     for a in range(0, TILE, 32):
         halves = [psi[:, 0, 0, a + h : a + h + 16].reshape(PHYS * 16, TILE) for h in (0, 16)]
         columns = jnp.concatenate(halves, 1)
-        columns = jnp.where(live, columns, jnp.zeros_like(columns))
         for m in range(0, TERMS * PHYS, 16):
             product = jnp.dot(
                 wide[m * 16 : (m + 16) * 16], columns, preferred_element_type=jnp.float32
@@ -143,14 +142,17 @@
     def ready():
         pl.when(slot == 0)(copy.wait)
 
-    live = slot < live_count[0]
-    left_slot(live, pattern, wide, kept, ready, psi, part, slot, mixed)
+    @pl.when(jnp.logical_or(slot == 0, slot < live_count[0]))
+    def _():
+        left_slot(pattern, wide, kept, ready, psi, part, slot, mixed)
 
 
 def left_second(first, pattern, live_count, wide, left, psi, before, part, mixed):
     slot = pl.program_id(0)
-    live = slot + first < live_count[0]
-    left_slot(live, pattern, wide, left, lambda: None, psi, part, slot, mixed)
+
+    @pl.when(slot + first < live_count[0])
+    def _():
+        left_slot(pattern, wide, left, lambda: None, psi, part, slot, mixed)
 
 
 def part_shape(count):
@@ -269,12 +271,17 @@
             numerator += jnp.sum(bra * value, 0)
             denominator += jnp.sum(bra * bra, 0)
         total[0] += numerator
-        total[1] += denominator * jnp.where(live, 0.25, 0.0)
+        total[1] += denominator * 0.25
         turn(following)
 
     split = part_a.shape[0]
-    pl.when(slot < split)(lambda: block(part_a, jnp.minimum(slot, split - 1)))
-    pl.when(slot >= split)(lambda: block(part_b, jnp.maximum(slot - split, 0)))
+    pl.when(jnp.logical_and(live, slot < split))(lambda: block(part_a, jnp.minimum(slot, split - 1)))
+    pl.when(jnp.logical_and(live, slot >= split))(lambda: block(part_b, jnp.maximum(slot - split, 0)))
+
+    @pl.when(jnp.logical_not(live))
+    def _():
+        for out in outs:
+            out[:, slot] = jnp.zeros((QUARTER, TILE, TILE), jnp.bfloat16)
 
     @pl.when(slot == SLOTS - 1)
     def _():

time: 67.6 us -> 66.8 us (0.988)
  Pallas kernels: 25.9 us -> 22.1 us
  blocking collectives: 25.9 us -> 28.2 us
  waiting for transfers between devices: 0.02 us -> 1.23 us
    pallas_call x1, Pallas kernels: 7.09 us -> 4.52 us  [left_late(): pl.pallas_call(functools.partial(left_second, first), grid_spec=pltpu.Pre...]
    all_to_all x1, blocking collectives: 25.9 us -> 28.2 us  [body(): sums = lax.all_to_all(sums, ('blk', 'mpo'), 0, 0, tiled=True)]
    pallas_call x1, Pallas kernels: 7.82 us -> 6.61 us  [right_product(): pl.pallas_call(right_kernel, grid_spec=pltpu.PrefetchScalarGridSpec(num_s...]
    ppermute x6, waiting for transfers between devices: 0.02 us -> 1.22 us  [trade(): return lax.ppermute(value, 'blk', pairs)]
  transfers between devices with their start and end apart: 9 -> 9, of which waited for: 0 -> 1; matrix products, arithmetic and copies ran while one was open for 0% -> 0% of each run, Pallas kernels for 23% -> 19%
where the time goes in v4:
time: 66.8 us; the launch traced here: 66.6 us
  blocking collectives  28.2 us (42%)
  Pallas kernels  22.1 us (33%)
  starting transfers between devices  13.8 us (21%)
  between operations  1.38 us (2%)
  waiting for transfers between devices  1.23 us (2%)
    all_to_all x1, blocking collectives, body(): sums = lax.all_to_all(sums, ('blk', 'mpo'), 0, 0, tiled=True)  28.2 us
    ppermute x6, starting transfers between devices, trade(): return lax.ppermute(value, 'blk', pairs)  8.7 us
    pallas_call x1, Pallas kernels, left_early(): pl.pallas_call(left_first, grid_spec=pltpu.PrefetchScalarGridSpec(num_sca...  8.12 us
    pallas_call x1, Pallas kernels, right_product(): pl.pallas_call(right_kernel, grid_spec=pltpu.PrefetchScalarGridSpec(num_s...  6.61 us
    ppermute x3, starting transfers between devices, shift(): lax.ppermute(value, axis, [(s, (s + steps) % count) for s in range(count)])  5.06 us
    pallas_call x1, Pallas kernels, left_late(): pl.pallas_call(functools.partial(left_second, first), grid_spec=pltpu.Pre...  4.52 us
    pallas_call x1, Pallas kernels, last(): pl.pallas_call(last_kernel, grid=(SLOTS // 2,), in_specs=[pl.BlockSpec(me...  1.87 us
  transfers between devices with their start and end apart: 9, of which 1 were waited for; matrix products, arithmetic and copies ran while one was open for 0% of the time, Pallas kernels for 19%

profile of v4, /device:TPU:1, one launch (start us, length us, event | category | flops | bytes accessed | tf_op | source)
XLA Modules:
  0.0 66.6 jit_solution(12432130535702428713)
XLA Ops:
  0.6 1.0 %shard_map.95.p0 = bf16[8,128,128]{2,1,0:T(8,128)(2,1)S(1)} custom-call(bf16[1,32,128,128]{3,2,1,0:T(8,128)(2,1)} %environment.1), custom_call_target="tpu_custom_call" | custom-call | tf_op jit(solution)/shard_map/pallas_call | solution.py:84
  1.6 3.3 %collective-permute-start.2 = (bf16[8,128,128]{2,1,0:T(8,128)(2,1)S(1)}, bf16[8,128,128]{2,1,0:T(8,128)(2,1)S(1)}, u32[]{:S(2)}, u32[]{:S(2)}) collective-permute-start(bf16[8,128,128]{2,1,0:T(8,128)(2,1)S(1)} %shard_map.95.p0), channel_id=1, source_target_pairs={{0,4},{4,0},{8,12},{12,8},{16,20},{20,16},{24,28},{28,24},{32,36},... | collective-permute-start | bytes 786440 | tf_op jit(solution)/shard_map/ppermute | solution.py:34
  4.9 0.7 collective-permute-start.1
  5.6 2.0 %collective-permute-start = (bf16[8,128,128]{2,1,0:T(8,128)(2,1)S(1)}, bf16[8,128,128]{2,1,0:T(8,128)(2,1)S(1)}, u32[]{:S(2)}, u32[]{:S(2)}) collective-permute-start(bf16[8,128,128]{2,1,0:T(8,128)(2,1)S(1)} %shard_map.95.p0), channel_id=1, source_target_pairs={{0,8},{4,12},{8,0},{12,4},{16,24},{20,28},{24,16},{28,20},{32,40},... | collective-permute-start | bytes 786440 | tf_op jit(solution)/shard_map/ppermute | solution.py:34
  8.3 8.1 %shard_map.94 = (bf16[2,16,128,1024]{3,2,1,0:T(8,128)(2,1)S(1)}, f32[8,128]{1,0:T(8,128)S(1)}, bf16[2048,256]{1,0:T(8,128)(2,1)S(1)}, bf16[32,128,128]{2,1,0:T(8,128)(2,1)S(1)}) custom-call(s32[2,8]{1,0:T(2,128)} %bitcast.4, s32[1]{0:T(128)S(6)} %copy.10.live_count, bf16[8,16,16]{2,1,0:T(8,128)(2,1)} %op.1, bf16[32,128,128]{2,1,0:T(8,128)(2,1)} %bitcast.3, ...), custom_call_target="tpu_custom_call" | custom-call | flops 6442450944 | bytes 2097152 | tf_op jit(solution)/shard_map/pallas_call | solution.py:169
  16.4 0.0 collective-permute-done.1.two.p3
  16.4 0.0 collective-permute-done.one.p2
  16.4 0.7 %collective-permute-start.3 = (bf16[8,128,128]{2,1,0:T(8,128)(2,1)S(1)}, bf16[8,128,128]{2,1,0:T(8,128)(2,1)S(1)}, u32[]{:S(2)}, u32[]{:S(2)}) collective-permute-start(bf16[8,128,128]{2,1,0:T(8,128)(2,1)S(1)} %collective-permute-done.one.p2), channel_id=1, source_target_pairs={{0,4},{4,0},{8,12},{12,8},{16,20},{20,16},{24,28},{28,24},{32,36},... | collective-permute-start | bytes 786440 | tf_op jit(solution)/shard_map/ppermute | solution.py:34
  17.1 0.1 collective-permute-start.4
  17.2 1.9 %collective-permute-start.5 = (bf16[8,128,128]{2,1,0:T(8,128)(2,1)S(1)}, bf16[8,128,128]{2,1,0:T(8,128)(2,1)S(1)}, u32[]{:S(2)}, u32[]{:S(2)}) collective-permute-start(bf16[8,128,128]{2,1,0:T(8,128)(2,1)S(1)} %shard_map.97), channel_id=1, source_target_pairs={{4,8},{8,4},{12,16},{16,12},{20,24},{24,20},{28,32},{32,28},{36,40... | collective-permute-start | bytes 786440 | tf_op jit(solution)/shard_map/ppermute | solution.py:34
  19.1 0.0 copy-start
  19.2 4.5 %shard_map.96.part_b = bf16[2,16,128,1024]{3,2,1,0:T(8,128)(2,1)S(1)} custom-call(s32[2,8]{1,0:T(2,128)} %bitcast.5, s32[1]{0:T(128)S(6)} %copy.10.live_count, bf16[2048,256]{1,0:T(8,128)(2,1)S(1)} %get-tuple-element.20.wide, bf16[32,128,128]{2,1,0:T(8,128)(2,1)S(1)} %get-tuple-element.21.left, bf16[16,1,4,128,128]{4,3,2,1,0:T(8,128)(2,1)} %psi.5, ...), custom_call_target="tpu_custom_call" | custom-call | flops 6442450944 | bytes 2097152 | tf_op jit(solution)/shard_map/pallas_call | solution.py:197
  23.7 0.0 collective-permute-done.2.p1
  23.7 1.2 %collective-permute-done.5.p6 = bf16[8,128,128]{2,1,0:T(8,128)(2,1)S(1)} collective-permute-done((bf16[8,128,128]{2,1,0:T(8,128)(2,1)S(1)}, bf16[8,128,128]{2,1,0:T(8,128)(2,1)S(1)}, u32[]{:S(2)}, u32[]{:S(2)}) %collective-permute-start.5) | collective-permute-done | bytes 262176 | tf_op jit(solution)/shard_map/ppermute | solution.py:34
  24.9 0.0 collective-permute-done.3.p4
  24.9 0.0 collective-permute-done.4.p5
  24.9 0.0 copy-done
  24.9 6.6 %shard_map.98 = (bf16[4,4,128,128]{3,2,1,0:T(8,128)(2,1)S(1)}, bf16[4,4,128,128]{3,2,1,0:T(8,128)(2,1)S(1)}, bf16[4,4,128,128]{3,2,1,0:T(8,128)(2,1)S(1)}, bf16[...) custom-call(s32[2,8]{1,0:T(2,128)} %bitcast.6, ...), custom_call_target="tpu_custom_call" | custom-call | flops 6442450944 | bytes 5242880 | tf_op jit(solution)/shard_map/pallas_call | solution.py:294
  31.5 1.4 %collective-permute-start.6 = (bf16[4,4,128,128]{3,2,1,0:T(8,128)(2,1)S(1)}, bf16[4,4,128,128]{3,2,1,0:T(8,128)(2,1)S(1)}, u32[]{:S(2)}, u32[]{:S(2)}) collective-permute-start(bf16[4,4,128,128]{3,2,1,0:T(8,128)(2,1)S(1)} %get-tuple-element.28), channel_id=1, source_target_pairs={{0,1},{1,2},{2,3},{3,0},{4,5},{5,6},{6,7},{7,4},{8,9},{9,10},{10,1... | collective-permute-start | bytes 1572872 | tf_op jit(solution)/shard_map/ppermute | solution.py:28
  32.9 2.6 %collective-permute-start.7 = (bf16[4,4,128,128]{3,2,1,0:T(8,128)(2,1)S(1)}, bf16[4,4,128,128]{3,2,1,0:T(8,128)(2,1)S(1)}, u32[]{:S(2)}, u32[]{:S(2)}) collective-permute-start(bf16[4,4,128,128]{3,2,1,0:T(8,128)(2,1)S(1)} %get-tuple-element.29), channel_id=1, source_target_pairs={{0,2},{1,3},{2,0},{3,1},{4,6},{5,7},{6,4},{7,5},{8,10},{9,11},{10,... | collective-permute-start | bytes 1572872 | tf_op jit(solution)/shard_map/ppermute | solution.py:28
  35.5 1.1 %collective-permute-start.8 = (bf16[4,4,128,128]{3,2,1,0:T(8,128)(2,1)S(1)}, bf16[4,4,128,128]{3,2,1,0:T(8,128)(2,1)S(1)}, u32[]{:S(2)}, u32[]{:S(2)}) collective-permute-start(bf16[4,4,128,128]{3,2,1,0:T(8,128)(2,1)S(1)} %get-tuple-element.30), channel_id=1, source_target_pairs={{0,3},{1,0},{2,1},{3,2},{4,7},{5,4},{6,5},{7,6},{8,11},{9,8},{10,9... | collective-permute-start | bytes 1572872 | tf_op jit(solution)/shard_map/ppermute | solution.py:28
  36.6 28.2 %all_to_all.5.sums = f32[256,1,128]{2,1,0:T(1,128)S(1)} all-to-all(f32[256,1,128]{2,1,0:T(1,128)S(1)} %get-tuple-element.26), channel_id=1, replica_groups=mesh['blk'=64,'mpo'=4] {'blk','mpo'}, dimensions={0} | all-to-all | bytes 262144 | tf_op jit(solution)/shard_map/all_to_all | solution.py:371
  64.8 0.0 collective-permute-done.6.r1
  64.8 0.0 collective-permute-done.7.r2
  64.8 0.0 collective-permute-done.8.r3
  64.8 1.9 %shard_map.99 = (bf16[4,1,4,128,128]{4,3,2,1,0:T(8,128)(2,1)}, bf16[4,1,4,128,128]{4,3,2,1,0:T(8,128)(2,1)}, f32[1,1]{1,0:T(1,128)}) custom-call(f32[256,1,128]{2,1,0:T(1,128)S(1)} %all_to_all.5.sums, bf16[4,4,128,128]{3,2,1,0:T(8,128)(2,1)S(1)} %get-tuple-element.27.o0, bf16[4,4,128,128]{3,2,1,0:T(8,128)(2,1)S(1)} %collective-permute-done.6.r1, ...), custom_call_target="tpu_custom_call" | custom-call | flops 1048576 | bytes 4194304 | tf_op jit(solution)/shard_map/pallas_call | solution.py:344
  (1 shorter events, 0.0 us)
Async XLA Ops:
  1.6 22.1 %collective-permute-start.2 = (bf16[8,128,128]{2,1,0:T(8,128)(2,1)S(1)}, bf16[8,128,128]{2,1,0:T(8,128)(2,1)S(1)}, u32[]{:S(2)}, u32[]{:S(2)}) collective-permute-start(bf16[8,128,128]{2,1,0:T(8,128)(2,1)S(1)} %shard_map.95.p0), channel_id=1, source_target_pairs={{0,4},{4,0},{8,12},{12,8},{16,20},{20,16},{24,28},{28,24},{32,36},... | collective-permute-start | bytes 786440 | tf_op jit(solution)/shard_map/ppermute | solution.py:34
  4.9 11.5 %collective-permute-start.1 = (bf16[8,128,128]{2,1,0:T(8,128)(2,1)S(1)}, bf16[8,128,128]{2,1,0:T(8,128)(2,1)S(1)}, u32[]{:S(2)}, u32[]{:S(2)}) collective-permute-start(bf16[8,128,128]{2,1,0:T(8,128)(2,1)S(1)} %shard_map.95.p0), channel_id=1, source_target_pairs={{8,16},{12,20},{16,8},{20,12},{24,32},{28,36},{32,24},{36,28},{40,... | collective-permute-start | bytes 786440 | tf_op jit(solution)/shard_map/ppermute | solution.py:34
  5.6 10.8 %collective-permute-start = (bf16[8,128,128]{2,1,0:T(8,128)(2,1)S(1)}, bf16[8,128,128]{2,1,0:T(8,128)(2,1)S(1)}, u32[]{:S(2)}, u32[]{:S(2)}) collective-permute-start(bf16[8,128,128]{2,1,0:T(8,128)(2,1)S(1)} %shard_map.95.p0), channel_id=1, source_target_pairs={{0,8},{4,12},{8,0},{12,4},{16,24},{20,28},{24,16},{28,20},{32,40},... | collective-permute-start | bytes 786440 | tf_op jit(solution)/shard_map/ppermute | solution.py:34
  16.4 8.5 %collective-permute-start.3 = (bf16[8,128,128]{2,1,0:T(8,128)(2,1)S(1)}, bf16[8,128,128]{2,1,0:T(8,128)(2,1)S(1)}, u32[]{:S(2)}, u32[]{:S(2)}) collective-permute-start(bf16[8,128,128]{2,1,0:T(8,128)(2,1)S(1)} %collective-permute-done.one.p2), channel_id=1, source_target_pairs={{0,4},{4,0},{8,12},{12,8},{16,20},{20,16},{24,28},{28,24},{32,36},... | collective-permute-start | bytes 786440 | tf_op jit(solution)/shard_map/ppermute | solution.py:34
  17.1 7.8 %collective-permute-start.4 = (bf16[8,128,128]{2,1,0:T(8,128)(2,1)S(1)}, bf16[8,128,128]{2,1,0:T(8,128)(2,1)S(1)}, u32[]{:S(2)}, u32[]{:S(2)}) collective-permute-start(bf16[8,128,128]{2,1,0:T(8,128)(2,1)S(1)} %collective-permute-done.1.two.p3), channel_id=1, source_target_pairs={{0,4},{4,0},{8,12},{12,8},{16,20},{20,16},{24,28},{28,24},{32,36},... | collective-permute-start | bytes 786440 | tf_op jit(solution)/shard_map/ppermute | solution.py:34
  17.2 7.7 %collective-permute-start.5 = (bf16[8,128,128]{2,1,0:T(8,128)(2,1)S(1)}, bf16[8,128,128]{2,1,0:T(8,128)(2,1)S(1)}, u32[]{:S(2)}, u32[]{:S(2)}) collective-permute-start(bf16[8,128,128]{2,1,0:T(8,128)(2,1)S(1)} %shard_map.97), channel_id=1, source_target_pairs={{4,8},{8,4},{12,16},{16,12},{20,24},{24,20},{28,32},{32,28},{36,40... | collective-permute-start | bytes 786440 | tf_op jit(solution)/shard_map/ppermute | solution.py:34
  19.1 5.8 %copy-start = (s32[1,4]{1,0:T(1,128)S(1)}, s32[1,4]{1,0:T(1,128)}, u32[]{:S(2)}) copy-start(s32[1,4]{1,0:T(1,128)} %right_sector.1) | copy-start | bytes 52
  31.5 33.2 %collective-permute-start.6 = (bf16[4,4,128,128]{3,2,1,0:T(8,128)(2,1)S(1)}, bf16[4,4,128,128]{3,2,1,0:T(8,128)(2,1)S(1)}, u32[]{:S(2)}, u32[]{:S(2)}) collective-permute-start(bf16[4,4,128,128]{3,2,1,0:T(8,128)(2,1)S(1)} %get-tuple-element.28), channel_id=1, source_target_pairs={{0,1},{1,2},{2,3},{3,0},{4,5},{5,6},{6,7},{7,4},{8,9},{9,10},{10,1... | collective-permute-start | bytes 1572872 | tf_op jit(solution)/shard_map/ppermute | solution.py:28
  32.9 31.9 %collective-permute-start.7 = (bf16[4,4,128,128]{3,2,1,0:T(8,128)(2,1)S(1)}, bf16[4,4,128,128]{3,2,1,0:T(8,128)(2,1)S(1)}, u32[]{:S(2)}, u32[]{:S(2)}) collective-permute-start(bf16[4,4,128,128]{3,2,1,0:T(8,128)(2,1)S(1)} %get-tuple-element.29), channel_id=1, source_target_pairs={{0,2},{1,3},{2,0},{3,1},{4,6},{5,7},{6,4},{7,5},{8,10},{9,11},{10,... | collective-permute-start | bytes 1572872 | tf_op jit(solution)/shard_map/ppermute | solution.py:28
  35.5 29.2 %collective-permute-start.8 = (bf16[4,4,128,128]{3,2,1,0:T(8,128)(2,1)S(1)}, bf16[4,4,128,128]{3,2,1,0:T(8,128)(2,1)S(1)}, u32[]{:S(2)}, u32[]{:S(2)}) collective-permute-start(bf16[4,4,128,128]{3,2,1,0:T(8,128)(2,1)S(1)} %get-tuple-element.30), channel_id=1, source_target_pairs={{0,3},{1,0},{2,1},{3,2},{4,7},{5,4},{6,5},{7,6},{8,11},{9,8},{10,9... | collective-permute-start | bytes 1572872 | tf_op jit(solution)/shard_map/ppermute | solution.py:28

commit v5 on v4

--- a/solution.py
+++ b/solution.py
@@ -321,32 +321,36 @@
     )
 
 
-def last_kernel(sums, o0, r1, r2, r3, ket, applied, residual, energy):
-    first = pl.program_id(0) * 2
-    lane = lax.broadcasted_iota(jnp.int32, (1, TILE), 1)
-    value = jnp.sum(sums[...], 0)
-    numerator = jnp.sum(jnp.where(lane == 0, value, 0.0), 1, keepdims=True)
-    denominator = jnp.sum(jnp.where(lane == TILE // 2, value, 0.0), 1, keepdims=True)
-    quotient = numerator / denominator
+def last_kernel(sums, o0, r1, r2, r3, ket, applied, residual, energy, quotient):
+    slot = pl.program_id(0)
+
+    @pl.when(slot == 0)
+    def _():
+        lane = lax.broadcasted_iota(jnp.int32, (1, TILE), 1)
+        value = jnp.sum(sums[...], 0)
+        numerator = jnp.sum(jnp.where(lane == 0, value, 0.0), 1, keepdims=True)
+        denominator = jnp.sum(jnp.where(lane == TILE // 2, value, 0.0), 1, keepdims=True)
+        quotient[...] = jnp.broadcast_to(numerator / denominator, quotient.shape)
+        energy[0, 0] = jnp.sum(numerator / denominator)
+
     for p in range(QUARTER):
-        for j in range(2):
-            result = sum(part[p, first + j].astype(jnp.float32) for part in (o0, r1, r2, r3))
-            result = result.astype(jnp.bfloat16)
-            applied[p, 0, j] = result
-            rest = result.astype(jnp.float32) - quotient * ket[p, first + j].astype(jnp.float32)
-            residual[p, 0, j] = rest.astype(jnp.bfloat16)
-    energy[0, 0] = jnp.sum(quotient)
+        result = sum(part[p, slot].astype(jnp.float32) for part in (o0, r1, r2, r3))
+        result = result.astype(jnp.bfloat16)
+        applied[p, 0, 0] = result
+        rest = result.astype(jnp.float32) - quotient[...] * ket[p, slot].astype(jnp.float32)
+        residual[p, 0, 0] = rest.astype(jnp.bfloat16)
 
 
 def last(sums, parts, ket):
-    result = pl.BlockSpec((QUARTER, 1, 2, TILE, TILE), lambda j: (0, 0, j, 0, 0))
+    result = pl.BlockSpec((QUARTER, 1, 1, TILE, TILE), lambda j: (0, 0, j, 0, 0))
     out = jax.ShapeDtypeStruct((QUARTER, 1, SLOTS, TILE, TILE), jnp.bfloat16)
     return pl.pallas_call(
         last_kernel,
-        grid=(SLOTS // 2,),
-        in_specs=[pl.BlockSpec(memory_space=pltpu.VMEM)] * 6,
+        grid=(SLOTS,),
+        in_specs=[RESIDENT] * 6,
         out_specs=[result, result, pl.BlockSpec(memory_space=pltpu.SMEM)],
         out_shape=[out, out, jax.ShapeDtypeStruct((1, 1), jnp.float32)],
+        scratch_shapes=[pltpu.VMEM((1, TILE), jnp.float32)],
         compiler_params=pltpu.CompilerParams(vmem_limit_bytes=16 << 20),
         cost_estimate=pl.CostEstimate(flops=1 << 20, bytes_accessed=4 << 20, transcendentals=0),
     )(*map(in_vmem, (sums, *parts, ket)))

time: 66.8 us -> 66.8 us (level)
  no operation moved by 1% of the time
where the time goes in v5:
time: 66.8 us; the launch traced here: 66.3 us
  blocking collectives  27.6 us (41%)
  Pallas kernels  22.4 us (34%)
  starting transfers between devices  13.6 us (20%)
  between operations  1.4 us (2%)
  waiting for transfers between devices  1.23 us (2%)
    all_to_all x1, blocking collectives, body(): sums = lax.all_to_all(sums, ('blk', 'mpo'), 0, 0, tiled=True)  27.6 us
    ppermute x6, starting transfers between devices, trade(): return lax.ppermute(value, 'blk', pairs)  8.56 us
    pallas_call x1, Pallas kernels, left_early(): pl.pallas_call(left_first, grid_spec=pltpu.PrefetchScalarGridSpec(num_sca...  8.12 us
    pallas_call x1, Pallas kernels, right_product(): pl.pallas_call(right_kernel, grid_spec=pltpu.PrefetchScalarGridSpec(num_s...  6.61 us
    ppermute x3, starting transfers between devices, shift(): lax.ppermute(value, axis, [(s, (s + steps) % count) for s in range(count)])  5.07 us
    pallas_call x1, Pallas kernels, left_late(): pl.pallas_call(functools.partial(left_second, first), grid_spec=pltpu.Pre...  4.53 us
    pallas_call x1, Pallas kernels, last(): pl.pallas_call(last_kernel, grid=(SLOTS,), in_specs=[RESIDENT] * 6, out_s...  2.17 us
  transfers between devices with their start and end apart: 9, of which 1 were waited for; matrix products, arithmetic and copies ran while one was open for 0% of the time, Pallas kernels for 19%

profile of v5, /device:TPU:1, one launch (start us, length us, event | category | flops | bytes accessed | tf_op | source)
XLA Modules:
  0.0 66.3 jit_solution(9238241818991941617)
XLA Ops:
  0.6 1.0 %shard_map.95.p0 = bf16[8,128,128]{2,1,0:T(8,128)(2,1)S(1)} custom-call(bf16[1,32,128,128]{3,2,1,0:T(8,128)(2,1)} %environment.1), custom_call_target="tpu_custom_call" | custom-call | tf_op jit(solution)/shard_map/pallas_call | solution.py:84
  1.6 3.3 %collective-permute-start.2 = (bf16[8,128,128]{2,1,0:T(8,128)(2,1)S(1)}, bf16[8,128,128]{2,1,0:T(8,128)(2,1)S(1)}, u32[]{:S(2)}, u32[]{:S(2)}) collective-permute-start(bf16[8,128,128]{2,1,0:T(8,128)(2,1)S(1)} %shard_map.95.p0), channel_id=1, source_target_pairs={{0,4},{4,0},{8,12},{12,8},{16,20},{20,16},{24,28},{28,24},{32,36},... | collective-permute-start | bytes 786440 | tf_op jit(solution)/shard_map/ppermute | solution.py:34
  4.9 0.7 %collective-permute-start.1 = (bf16[8,128,128]{2,1,0:T(8,128)(2,1)S(1)}, bf16[8,128,128]{2,1,0:T(8,128)(2,1)S(1)}, u32[]{:S(2)}, u32[]{:S(2)}) collective-permute-start(bf16[8,128,128]{2,1,0:T(8,128)(2,1)S(1)} %shard_map.95.p0), channel_id=1, source_target_pairs={{8,16},{12,20},{16,8},{20,12},{24,32},{28,36},{32,24},{36,28},{40,... | collective-permute-start | bytes 786440 | tf_op jit(solution)/shard_map/ppermute | solution.py:34
  5.6 2.0 %collective-permute-start = (bf16[8,128,128]{2,1,0:T(8,128)(2,1)S(1)}, bf16[8,128,128]{2,1,0:T(8,128)(2,1)S(1)}, u32[]{:S(2)}, u32[]{:S(2)}) collective-permute-start(bf16[8,128,128]{2,1,0:T(8,128)(2,1)S(1)} %shard_map.95.p0), channel_id=1, source_target_pairs={{0,8},{4,12},{8,0},{12,4},{16,24},{20,28},{24,16},{28,20},{32,40},... | collective-permute-start | bytes 786440 | tf_op jit(solution)/shard_map/ppermute | solution.py:34
  8.3 8.1 %shard_map.94 = (bf16[2,16,128,1024]{3,2,1,0:T(8,128)(2,1)S(1)}, f32[8,128]{1,0:T(8,128)S(1)}, bf16[2048,256]{1,0:T(8,128)(2,1)S(1)}, bf16[32,128,128]{2,1,0:T(8,128)(2,1)S(1)}) custom-call(s32[2,8]{1,0:T(2,128)} %bitcast.4, s32[1]{0:T(128)S(6)} %copy.10.live_count, bf16[8,16,16]{2,1,0:T(8,128)(2,1)} %op.1, bf16[32,128,128]{2,1,0:T(8,128)(2,1)} %bitcast.3, ...), custom_call_target="tpu_custom_call" | custom-call | flops 6442450944 | bytes 2097152 | tf_op jit(solution)/shard_map/pallas_call | solution.py:169
  16.4 0.0 collective-permute-done.1.two.p3
  16.4 0.0 collective-permute-done.one.p2
  16.4 0.1 collective-permute-start.3
  16.6 0.6 collective-permute-start.4
  17.1 1.9 %collective-permute-start.5 = (bf16[8,128,128]{2,1,0:T(8,128)(2,1)S(1)}, bf16[8,128,128]{2,1,0:T(8,128)(2,1)S(1)}, u32[]{:S(2)}, u32[]{:S(2)}) collective-permute-start(bf16[8,128,128]{2,1,0:T(8,128)(2,1)S(1)} %shard_map.97), channel_id=1, source_target_pairs={{4,8},{8,4},{12,16},{16,12},{20,24},{24,20},{28,32},{32,28},{36,40... | collective-permute-start | bytes 786440 | tf_op jit(solution)/shard_map/ppermute | solution.py:34
  19.0 0.0 copy-start
  19.1 4.5 %shard_map.96.part_b = bf16[2,16,128,1024]{3,2,1,0:T(8,128)(2,1)S(1)} custom-call(s32[2,8]{1,0:T(2,128)} %bitcast.5, s32[1]{0:T(128)S(6)} %copy.10.live_count, bf16[2048,256]{1,0:T(8,128)(2,1)S(1)} %get-tuple-element.20.wide, bf16[32,128,128]{2,1,0:T(8,128)(2,1)S(1)} %get-tuple-element.21.left, bf16[16,1,4,128,128]{4,3,2,1,0:T(8,128)(2,1)} %psi.5, ...), custom_call_target="tpu_custom_call" | custom-call | flops 6442450944 | bytes 2097152 | tf_op jit(solution)/shard_map/pallas_call | solution.py:197
  23.6 0.0 collective-permute-done.2.p1
  23.6 1.2 %collective-permute-done.5.p6 = bf16[8,128,128]{2,1,0:T(8,128)(2,1)S(1)} collective-permute-done((bf16[8,128,128]{2,1,0:T(8,128)(2,1)S(1)}, bf16[8,128,128]{2,1,0:T(8,128)(2,1)S(1)}, u32[]{:S(2)}, u32[]{:S(2)}) %collective-permute-start.5) | collective-permute-done | bytes 262176 | tf_op jit(solution)/shard_map/ppermute | solution.py:34
  24.8 0.0 collective-permute-done.3.p4
  24.8 0.0 collective-permute-done.4.p5
  24.8 0.0 copy-done
  24.8 6.6 %shard_map.98 = (bf16[4,4,128,128]{3,2,1,0:T(8,128)(2,1)S(1)}, bf16[4,4,128,128]{3,2,1,0:T(8,128)(2,1)S(1)}, bf16[4,4,128,128]{3,2,1,0:T(8,128)(2,1)S(1)}, bf16[...) custom-call(s32[2,8]{1,0:T(2,128)} %bitcast.6, ...), custom_call_target="tpu_custom_call" | custom-call | flops 6442450944 | bytes 5242880 | tf_op jit(solution)/shard_map/pallas_call | solution.py:294
  31.4 1.4 %collective-permute-start.6 = (bf16[4,4,128,128]{3,2,1,0:T(8,128)(2,1)S(1)}, bf16[4,4,128,128]{3,2,1,0:T(8,128)(2,1)S(1)}, u32[]{:S(2)}, u32[]{:S(2)}) collective-permute-start(bf16[4,4,128,128]{3,2,1,0:T(8,128)(2,1)S(1)} %get-tuple-element.28), channel_id=1, source_target_pairs={{0,1},{1,2},{2,3},{3,0},{4,5},{5,6},{6,7},{7,4},{8,9},{9,10},{10,1... | collective-permute-start | bytes 1572872 | tf_op jit(solution)/shard_map/ppermute | solution.py:28
  32.8 2.6 %collective-permute-start.7 = (bf16[4,4,128,128]{3,2,1,0:T(8,128)(2,1)S(1)}, bf16[4,4,128,128]{3,2,1,0:T(8,128)(2,1)S(1)}, u32[]{:S(2)}, u32[]{:S(2)}) collective-permute-start(bf16[4,4,128,128]{3,2,1,0:T(8,128)(2,1)S(1)} %get-tuple-element.29), channel_id=1, source_target_pairs={{0,2},{1,3},{2,0},{3,1},{4,6},{5,7},{6,4},{7,5},{8,10},{9,11},{10,... | collective-permute-start | bytes 1572872 | tf_op jit(solution)/shard_map/ppermute | solution.py:28
  35.4 1.1 %collective-permute-start.8 = (bf16[4,4,128,128]{3,2,1,0:T(8,128)(2,1)S(1)}, bf16[4,4,128,128]{3,2,1,0:T(8,128)(2,1)S(1)}, u32[]{:S(2)}, u32[]{:S(2)}) collective-permute-start(bf16[4,4,128,128]{3,2,1,0:T(8,128)(2,1)S(1)} %get-tuple-element.30), channel_id=1, source_target_pairs={{0,3},{1,0},{2,1},{3,2},{4,7},{5,4},{6,5},{7,6},{8,11},{9,8},{10,9... | collective-permute-start | bytes 1572872 | tf_op jit(solution)/shard_map/ppermute | solution.py:28
  36.5 27.6 %all_to_all.5.sums = f32[256,1,128]{2,1,0:T(1,128)S(1)} all-to-all(f32[256,1,128]{2,1,0:T(1,128)S(1)} %get-tuple-element.26), channel_id=1, replica_groups=mesh['blk'=64,'mpo'=4] {'blk','mpo'}, dimensions={0} | all-to-all | bytes 262144 | tf_op jit(solution)/shard_map/all_to_all | solution.py:375
  64.1 0.0 collective-permute-done.6.r1
  64.1 0.0 collective-permute-done.7.r2
  64.1 0.0 collective-permute-done.8.r3
  64.1 2.2 %shard_map.99 = (bf16[4,1,4,128,128]{4,3,2,1,0:T(8,128)(2,1)}, bf16[4,1,4,128,128]{4,3,2,1,0:T(8,128)(2,1)}, f32[1,1]{1,0:T(1,128)}) custom-call(f32[256,1,128]{2,1,0:T(1,128)S(1)} %all_to_all.5.sums, bf16[4,4,128,128]{3,2,1,0:T(8,128)(2,1)S(1)} %get-tuple-element.27.o0, bf16[4,4,128,128]{3,2,1,0:T(8,128)(2,1)S(1)} %collective-permute-done.6.r1, ...), custom_call_target="tpu_custom_call" | custom-call | flops 1048576 | bytes 4194304 | tf_op jit(solution)/shard_map/pallas_call | solution.py:347
  (1 shorter events, 0.0 us)
Async XLA Ops:
  1.6 22.0 %collective-permute-start.2 = (bf16[8,128,128]{2,1,0:T(8,128)(2,1)S(1)}, bf16[8,128,128]{2,1,0:T(8,128)(2,1)S(1)}, u32[]{:S(2)}, u32[]{:S(2)}) collective-permute-start(bf16[8,128,128]{2,1,0:T(8,128)(2,1)S(1)} %shard_map.95.p0), channel_id=1, source_target_pairs={{0,4},{4,0},{8,12},{12,8},{16,20},{20,16},{24,28},{28,24},{32,36},... | collective-permute-start | bytes 786440 | tf_op jit(solution)/shard_map/ppermute | solution.py:34
  4.9 11.5 %collective-permute-start.1 = (bf16[8,128,128]{2,1,0:T(8,128)(2,1)S(1)}, bf16[8,128,128]{2,1,0:T(8,128)(2,1)S(1)}, u32[]{:S(2)}, u32[]{:S(2)}) collective-permute-start(bf16[8,128,128]{2,1,0:T(8,128)(2,1)S(1)} %shard_map.95.p0), channel_id=1, source_target_pairs={{8,16},{12,20},{16,8},{20,12},{24,32},{28,36},{32,24},{36,28},{40,... | collective-permute-start | bytes 786440 | tf_op jit(solution)/shard_map/ppermute | solution.py:34
  5.6 10.8 %collective-permute-start = (bf16[8,128,128]{2,1,0:T(8,128)(2,1)S(1)}, bf16[8,128,128]{2,1,0:T(8,128)(2,1)S(1)}, u32[]{:S(2)}, u32[]{:S(2)}) collective-permute-start(bf16[8,128,128]{2,1,0:T(8,128)(2,1)S(1)} %shard_map.95.p0), channel_id=1, source_target_pairs={{0,8},{4,12},{8,0},{12,4},{16,24},{20,28},{24,16},{28,20},{32,40},... | collective-permute-start | bytes 786440 | tf_op jit(solution)/shard_map/ppermute | solution.py:34
  16.4 8.4 %collective-permute-start.3 = (bf16[8,128,128]{2,1,0:T(8,128)(2,1)S(1)}, bf16[8,128,128]{2,1,0:T(8,128)(2,1)S(1)}, u32[]{:S(2)}, u32[]{:S(2)}) collective-permute-start(bf16[8,128,128]{2,1,0:T(8,128)(2,1)S(1)} %collective-permute-done.one.p2), channel_id=1, source_target_pairs={{0,4},{4,0},{8,12},{12,8},{16,20},{20,16},{24,28},{28,24},{32,36},... | collective-permute-start | bytes 786440 | tf_op jit(solution)/shard_map/ppermute | solution.py:34
  16.6 8.2 %collective-permute-start.4 = (bf16[8,128,128]{2,1,0:T(8,128)(2,1)S(1)}, bf16[8,128,128]{2,1,0:T(8,128)(2,1)S(1)}, u32[]{:S(2)}, u32[]{:S(2)}) collective-permute-start(bf16[8,128,128]{2,1,0:T(8,128)(2,1)S(1)} %collective-permute-done.1.two.p3), channel_id=1, source_target_pairs={{0,4},{4,0},{8,12},{12,8},{16,20},{20,16},{24,28},{28,24},{32,36},... | collective-permute-start | bytes 786440 | tf_op jit(solution)/shard_map/ppermute | solution.py:34
  17.1 7.7 %collective-permute-start.5 = (bf16[8,128,128]{2,1,0:T(8,128)(2,1)S(1)}, bf16[8,128,128]{2,1,0:T(8,128)(2,1)S(1)}, u32[]{:S(2)}, u32[]{:S(2)}) collective-permute-start(bf16[8,128,128]{2,1,0:T(8,128)(2,1)S(1)} %shard_map.97), channel_id=1, source_target_pairs={{4,8},{8,4},{12,16},{16,12},{20,24},{24,20},{28,32},{32,28},{36,40... | collective-permute-start | bytes 786440 | tf_op jit(solution)/shard_map/ppermute | solution.py:34
  19.0 5.8 %copy-start = (s32[1,4]{1,0:T(1,128)S(1)}, s32[1,4]{1,0:T(1,128)}, u32[]{:S(2)}) copy-start(s32[1,4]{1,0:T(1,128)} %right_sector.1) | copy-start | bytes 52
  31.4 32.6 %collective-permute-start.6 = (bf16[4,4,128,128]{3,2,1,0:T(8,128)(2,1)S(1)}, bf16[4,4,128,128]{3,2,1,0:T(8,128)(2,1)S(1)}, u32[]{:S(2)}, u32[]{:S(2)}) collective-permute-start(bf16[4,4,128,128]{3,2,1,0:T(8,128)(2,1)S(1)} %get-tuple-element.28), channel_id=1, source_target_pairs={{0,1},{1,2},{2,3},{3,0},{4,5},{5,6},{6,7},{7,4},{8,9},{9,10},{10,1... | collective-permute-start | bytes 1572872 | tf_op jit(solution)/shard_map/ppermute | solution.py:28
  32.8 31.3 %collective-permute-start.7 = (bf16[4,4,128,128]{3,2,1,0:T(8,128)(2,1)S(1)}, bf16[4,4,128,128]{3,2,1,0:T(8,128)(2,1)S(1)}, u32[]{:S(2)}, u32[]{:S(2)}) collective-permute-start(bf16[4,4,128,128]{3,2,1,0:T(8,128)(2,1)S(1)} %get-tuple-element.29), channel_id=1, source_target_pairs={{0,2},{1,3},{2,0},{3,1},{4,6},{5,7},{6,4},{7,5},{8,10},{9,11},{10,... | collective-permute-start | bytes 1572872 | tf_op jit(solution)/shard_map/ppermute | solution.py:28
  35.4 28.6 %collective-permute-start.8 = (bf16[4,4,128,128]{3,2,1,0:T(8,128)(2,1)S(1)}, bf16[4,4,128,128]{3,2,1,0:T(8,128)(2,1)S(1)}, u32[]{:S(2)}, u32[]{:S(2)}) collective-permute-start(bf16[4,4,128,128]{3,2,1,0:T(8,128)(2,1)S(1)} %get-tuple-element.30), channel_id=1, source_target_pairs={{0,3},{1,0},{2,1},{3,2},{4,7},{5,4},{6,5},{7,6},{8,11},{9,8},{10,9... | collective-permute-start | bytes 1572872 | tf_op jit(solution)/shard_map/ppermute | solution.py:28
